TPU v7x, 128 devices: a whole 4x4x4 slice. The times are simulated.
128 devices in a mesh: snd: 16 (over x, z), cell: 8 (over y, core).
Axes of the slice: x: 4, y: 4, z: 4, core: 2. Of those that a mesh axis runs over, the one named last changes fastest.
Arguments:
- probes: bfloat16 [1024, 4, 32, 128], P(('snd', 'cell')), may hold values from -6 to 6
- spatial: bfloat16 [1024, 128, 128], P(('snd', 'cell')), may hold values from -0.5 to 0.5
- rho: float32 [1024], P(('snd', 'cell')), may hold values from 0.3 to 0.9
- foot_tile: int32 [16384, 4], P('snd'), may hold values from 0 to 1023, all different within a row; in each aligned block of 1024 rows (0 to 1023, 1024 to 2047, ...) at most 8 rows name the same one
- foot_week: int32 [16384, 4], P('snd'), may hold values from 0 to 3
- footprint: bfloat16 [16384, 4, 128], P('snd'), may hold values from 0.049804688 to 1
- sigma: float32 [16384], P('snd'), may hold values from 3 to 12
Outputs:
- probe_image: float32 [1024, 4, 32, 128], P(('snd', 'cell'))
- variance_drop: float32 [1024, 4, 128], P(('snd', 'cell'))
Inputs may be any that keep to these rules, and one draw needn't show every extreme that they name: `foot_tile`: the 4 tiles of one sounding differ. In every aligned block of 1024 soundings no tile is named by more than 8 soundings, a bound that some block reaches.
All inputs are finite; a program needn't handle non-finite values.
Results may differ from a plain program's by a relative error of at most 0.0037.
Values may be sent and summed in bfloat16 or wider, within the bound.
A program may use at most 128 MiB of HBM per device.

v0:
```python
import jax
import jax.numpy as jnp
from jax import lax
from jax.sharding import PartitionSpec as P


def prior_apply(probes, spatial, rho):
    spread = jnp.einsum("twpj,tij->twpi", probes, spatial, preferred_element_type=jnp.float32)
    week_count = probes.shape[1]
    running = spread[:, 0]
    stacked = [running]
    for week_step in range(1, week_count):
        running = spread[:, week_step] + rho[:, None, None] * running
        stacked.append(running)
    return jnp.stack(stacked, 1).astype(jnp.bfloat16)


def prior_adjoint(adjoint, spatial, rho):
    week_count = adjoint.shape[1]
    running = adjoint[:, week_count - 1]
    stacked = [running]
    for week_step in range(week_count - 2, -1, -1):
        running = adjoint[:, week_step] + rho[:, None, None] * running
        stacked.append(running)
    carried = jnp.stack(stacked[::-1], 1).astype(jnp.bfloat16)
    return jnp.einsum("twpi,tij->twpj", carried, spatial, preferred_element_type=jnp.float32)


def gather_forward(lookup, rowset, valid, shapes, probe_count, cell_count, block_rows):
    block_count = rowset.shape[0] // block_rows

    def forward(inputs):
        rows_here, valid_here, shape_here = inputs
        fetched = lookup[rows_here].reshape(block_rows, probe_count, cell_count)
        values_here = jnp.einsum(
            "epc,ec->ep", fetched, shape_here, preferred_element_type=jnp.float32
        )
        return jnp.where(valid_here[:, None], values_here, 0.0)

    safe_rows = jnp.where(valid, rowset, 0)
    results = lax.map(
        forward,
        (
            safe_rows.reshape(block_count, block_rows),
            valid.reshape(block_count, block_rows),
            shapes.reshape(block_count, block_rows, cell_count),
        ),
    )
    return results.reshape(-1, probe_count)


def scatter_adjoint(slot_count, rowset, valid, shapes, values, block_rows):
    block_count = rowset.shape[0] // block_rows
    cell_count = shapes.shape[1]
    probe_count = values.shape[1]
    drop_rows = jnp.where(valid, rowset, slot_count)

    def accumulate(summed_total, inputs):
        rows_here, shape_here, values_here = inputs
        contrib = (shape_here.astype(jnp.float32)[:, None, :] * values_here[:, :, None]).reshape(
            block_rows, probe_count * cell_count
        )
        return (summed_total.at[rows_here].add(contrib, mode="drop"), None)

    summed_total, _ = lax.scan(
        accumulate,
        jnp.zeros((slot_count, probe_count * cell_count), jnp.float32),
        (
            drop_rows.reshape(block_count, block_rows),
            shapes.reshape(block_count, block_rows, cell_count),
            values.reshape(block_count, block_rows, probe_count),
        ),
    )
    return summed_total


def weigh(partial_value, sigma):
    seen_sums = lax.psum(partial_value, "cell")
    weighted = seen_sums / (sigma * sigma)[:, None]
    return weighted


def per_device(probes, spatial, rho, foot_tile, foot_week, footprint, sigma):
    tiles_here, week_count, probe_count, cell_count = probes.shape
    snd_count = lax.axis_size("snd")
    cell_groups = lax.axis_size("cell")
    cell_index = lax.axis_index("cell")
    sound_here, per_sound = foot_tile.shape
    entries = sound_here * per_sound
    prior_field = prior_apply(probes, spatial, rho)
    tiles_flat = foot_tile.reshape(-1)
    weeks_flat = foot_week.reshape(-1)
    shapes = footprint.reshape(-1, cell_count)
    gathered = lax.all_gather(prior_field, "snd", axis=0, tiled=True)
    group_tiles = tiles_here * snd_count
    block_rows = min(1024, entries)
    tile_group = tiles_flat // tiles_here
    in_group = tile_group % cell_groups == cell_index
    rowset = (
        tile_group // cell_groups * tiles_here + tiles_flat % tiles_here
    ) * week_count + weeks_flat
    lookup = gathered.reshape(group_tiles * week_count, probe_count * cell_count)
    partial_value = gather_forward(
        lookup, rowset, in_group, shapes, probe_count, cell_count, block_rows
    )
    partial_value = partial_value.reshape(sound_here, per_sound, probe_count).sum(1)
    weighted = weigh(partial_value, sigma)
    entry_values = jnp.broadcast_to(
        weighted[:, None, :], (sound_here, per_sound, probe_count)
    ).reshape(entries, probe_count)
    adjoint_terms = scatter_adjoint(
        group_tiles * week_count, rowset, in_group, shapes, entry_values, block_rows
    )
    adjoint_terms = adjoint_terms.reshape(group_tiles, week_count, probe_count, cell_count)
    adjoint = lax.psum_scatter(adjoint_terms, "snd", scatter_dimension=0, tiled=True)
    probe_image = prior_adjoint(adjoint, spatial, rho)
    variance_drop = jnp.mean(probes.astype(jnp.float32) * probe_image, axis=2)
    return (probe_image, variance_drop)


def solution(mesh):
    placed = (
        P(("snd", "cell"), None, None, None),
        P(("snd", "cell"), None, None),
        P(("snd", "cell")),
        P("snd", None),
        P("snd", None),
        P("snd", None, None),
        P("snd"),
    )
    return jax.shard_map(
        per_device,
        mesh=mesh,
        in_specs=placed,
        out_specs=(P(("snd", "cell"), None, None, None), P(("snd", "cell"), None, None)),
        check_vma=False,
    )
```

profile of v0, /device:TPU:1, one launch (start us, length us, event | category | flops | bytes accessed | tf_op | source)
XLA Modules:
  0.0 604.7 jit_solution(11164680130079508935)
XLA Ops:
  8.1 1.2 fusion.14
  13.5 52.4 %all-gather.2.cloned.1.call-done = bf16[128,4,32,128]{3,2,1,0:T(8,128)(2,1)} async-done(((bf16[8,4,32,128]{3,2,1,0:T(8,128)(2,1)}), bf16[128,4,32,128]{3,2,1,0:T(8,128)(2,1)}) %all-gather.2.cloned.1.call-update) | async-done | bytes 4194320 | tf_op jit(solution)/shard_map/all_gather | solution.py:94
  66.0 8.3 %copy.29 = bf16[64,8,32,128]{3,1,2,0:T(8,128)(2,1)} copy(bf16[64,8,32,128]{3,2,1,0:T(8,128)(2,1)} %bitcast.83) | data formatting | bytes 8388608
  74.2 144.7 %while.20 = (s32[]{:T(128)}, f32[4,1024,32]{2,1,0:T(8,128)}, pred[4,1024]{1,0:T(4,128)(4,1)S(1)}, s32[4,1024]{1,0:T(4,128)S(1)}, bf16[512,4096]{1,0:T(8,128)(2,1)}, /*index=5*/bf16[4,1024,128]{2,1,0:T(8,128)(2,1)S(1)}, s32[]{:T(128)}) while((s32[]{:T(128)}, f32[4,1024,32]{2,1,0:T(8,128)}, pred[4,1024]{1,0:T(4,128)(4,1)S(1)}, ...), condition=%wide.region_1.2_spmd, body=%wide.region_0.1_spmd.sunk | while | flops 8425474 | bytes 43539556 | solution.py:41
  74.3 17.8 %gather_fusion = bf16[1024,4096]{1,0:T(8,128)(2,1)} fusion(bf16[512,4096]{1,0:T(8,128)(2,1)} %get-tuple-element.182, s32[1024]{0:T(1024)S(1)} %broadcast_clamp_fusion.2), kind=kCustom, calls=%fused_computation.clone.1 | custom fusion | bytes 16781312 | tf_op jit(solution)/shard_map/while/body/eval_jaxpr/gather | solution.py:34
  92.1 9.4 %copy.34 = bf16[128,8,32,128]{3,2,1,0:T(8,128)(2,1)} copy(bf16[128,8,32,128]{3,1,2,0:T(8,128)(2,1)} %bitcast.76) | data formatting | bytes 16777216 | tf_op jit(solution)/shard_map/while
  101.6 7.8 %fusion.40 = f32[1024,1,32]{2,1,0:T(1,128)S(1)} fusion(bf16[1024,32,128]{2,1,0:T(8,128)(2,1)} %bitcast.77, bf16[1024,128,1]{1,0,2:T(8,128)(2,1)S(1)} %dynamic-slice_bitcast_fusion.4), kind=kOutput, calls=%fused_computation.10.clone.1 | convolution fusion | flops 8388608 | bytes 8781824 | tf_op jit(solution)/shard_map/while/body/eval_jaxpr/epc,ec->ep/dot_general | solution.py:35
  110.5 17.8 %gather_fusion = bf16[1024,4096]{1,0:T(8,128)(2,1)} fusion(bf16[512,4096]{1,0:T(8,128)(2,1)} %get-tuple-element.182, s32[1024]{0:T(1024)S(1)} %broadcast_clamp_fusion.2), kind=kCustom, calls=%fused_computation.clone.1 | custom fusion | bytes 16781312 | tf_op jit(solution)/shard_map/while/body/eval_jaxpr/gather | solution.py:34
  128.3 9.4 %copy.34 = bf16[128,8,32,128]{3,2,1,0:T(8,128)(2,1)} copy(bf16[128,8,32,128]{3,1,2,0:T(8,128)(2,1)} %bitcast.76) | data formatting | bytes 16777216 | tf_op jit(solution)/shard_map/while
  137.7 7.8 %fusion.40 = f32[1024,1,32]{2,1,0:T(1,128)S(1)} fusion(bf16[1024,32,128]{2,1,0:T(8,128)(2,1)} %bitcast.77, bf16[1024,128,1]{1,0,2:T(8,128)(2,1)S(1)} %dynamic-slice_bitcast_fusion.4), kind=kOutput, calls=%fused_computation.10.clone.1 | convolution fusion | flops 8388608 | bytes 8781824 | tf_op jit(solution)/shard_map/while/body/eval_jaxpr/epc,ec->ep/dot_general | solution.py:35
  146.7 17.8 %gather_fusion = bf16[1024,4096]{1,0:T(8,128)(2,1)} fusion(bf16[512,4096]{1,0:T(8,128)(2,1)} %get-tuple-element.182, s32[1024]{0:T(1024)S(1)} %broadcast_clamp_fusion.2), kind=kCustom, calls=%fused_computation.clone.1 | custom fusion | bytes 16781312 | tf_op jit(solution)/shard_map/while/body/eval_jaxpr/gather | solution.py:34
  164.5 9.4 %copy.34 = bf16[128,8,32,128]{3,2,1,0:T(8,128)(2,1)} copy(bf16[128,8,32,128]{3,1,2,0:T(8,128)(2,1)} %bitcast.76) | data formatting | bytes 16777216 | tf_op jit(solution)/shard_map/while
  173.9 7.8 %fusion.40 = f32[1024,1,32]{2,1,0:T(1,128)S(1)} fusion(bf16[1024,32,128]{2,1,0:T(8,128)(2,1)} %bitcast.77, bf16[1024,128,1]{1,0,2:T(8,128)(2,1)S(1)} %dynamic-slice_bitcast_fusion.4), kind=kOutput, calls=%fused_computation.10.clone.1 | convolution fusion | flops 8388608 | bytes 8781824 | tf_op jit(solution)/shard_map/while/body/eval_jaxpr/epc,ec->ep/dot_general | solution.py:35
  182.8 17.8 %gather_fusion = bf16[1024,4096]{1,0:T(8,128)(2,1)} fusion(bf16[512,4096]{1,0:T(8,128)(2,1)} %get-tuple-element.182, s32[1024]{0:T(1024)S(1)} %broadcast_clamp_fusion.2), kind=kCustom, calls=%fused_computation.clone.1 | custom fusion | bytes 16781312 | tf_op jit(solution)/shard_map/while/body/eval_jaxpr/gather | solution.py:34
  200.6 9.4 %copy.34 = bf16[128,8,32,128]{3,2,1,0:T(8,128)(2,1)} copy(bf16[128,8,32,128]{3,1,2,0:T(8,128)(2,1)} %bitcast.76) | data formatting | bytes 16777216 | tf_op jit(solution)/shard_map/while
  210.1 7.8 %fusion.40 = f32[1024,1,32]{2,1,0:T(1,128)S(1)} fusion(bf16[1024,32,128]{2,1,0:T(8,128)(2,1)} %bitcast.77, bf16[1024,128,1]{1,0,2:T(8,128)(2,1)S(1)} %dynamic-slice_bitcast_fusion.4), kind=kOutput, calls=%fused_computation.10.clone.1 | convolution fusion | flops 8388608 | bytes 8781824 | tf_op jit(solution)/shard_map/while/body/eval_jaxpr/epc,ec->ep/dot_general | solution.py:35
  218.9 3.7 reduce_sum.18
  222.7 58.4 %all-reduce.2.cloned.1.call-done = f32[1024,32]{1,0:T(8,128)} async-done(((f32[1024,32]{1,0:T(8,128)}), f32[1024,32]{1,0:T(8,128)}) %all-reduce.2.cloned.1.call-update) | async-done | bytes 131088 | tf_op jit(solution)/shard_map/psum | solution.py:78
  281.1 1.2 broadcast_divide_fusion
  282.7 4.3 broadcast_in_dim.34
  286.9 214.0 %while.21 = (s32[]{:T(128)}, f32[512,4096]{1,0:T(8,128)}, s32[4,1024]{1,0:T(4,128)S(1)}, bf16[4,1024,128]{2,1,0:T(8,128)(2,1)S(1)}, f32[4,1024,32]{2,1,0:T(8,128)S(1)}, /*index=5*/s32[]{:T(128)}) while((s32[]{:T(128)}, f32[512,4096]{1,0:T(8,128)}, s32[4,1024]{1,0:T(4,128)S(1)}, bf16[4,1024,128]{2,1,0:T(8,128)(2,1)S(1)}, ...), condition=%wide.region_6.7_spmd, body=%wide.region_4.6_spmd.sunk | while | flops 8522754 | bytes 43655256 | solution.py:65
  287.1 9.4 %broadcast_multiply_fusion.3 = f32[1024,32,128]{2,1,0:T(8,128)} fusion(f32[1024,32]{1,0:T(8,128)S(1)} %dynamic-slice_bitcast_fusion.5, f32[1024,128]{1,0:T(8,128)S(1)} %bitcast_convert_fusion.2), kind=kLoop, calls=%fused_computation.5.clone.1 | loop fusion | flops 4194304 | bytes 17432576 | tf_op jit(solution)/shard_map/while/body/eval_jaxpr/mul | solution.py:60
  296.5 44.0 %scatter_custom_fusion.5 = f32[512,4096]{1,0:T(8,128)} fusion(f32[512,4096]{1,0:T(8,128)} %get-tuple-element.192, s32[1024]{0:T(1024)S(1)} %bitcast.86, f32[128,8,32,128]{3,2,1,0:T(8,128)} %bitcast.75), kind=kCustom, calls=%fused_computation.2.clone.1 | custom fusion | flops 4194304 | bytes 25165824 | tf_op jit(solution)/shard_map/while/body/eval_jaxpr/scatter-add | solution.py:63
  340.6 9.4 %broadcast_multiply_fusion.3 = f32[1024,32,128]{2,1,0:T(8,128)} fusion(f32[1024,32]{1,0:T(8,128)S(1)} %dynamic-slice_bitcast_fusion.5, f32[1024,128]{1,0:T(8,128)S(1)} %bitcast_convert_fusion.2), kind=kLoop, calls=%fused_computation.5.clone.1 | loop fusion | flops 4194304 | bytes 17432576 | tf_op jit(solution)/shard_map/while/body/eval_jaxpr/mul | solution.py:60
  349.9 44.0 %scatter_custom_fusion.5 = f32[512,4096]{1,0:T(8,128)} fusion(f32[512,4096]{1,0:T(8,128)} %get-tuple-element.192, s32[1024]{0:T(1024)S(1)} %bitcast.86, f32[128,8,32,128]{3,2,1,0:T(8,128)} %bitcast.75), kind=kCustom, calls=%fused_computation.2.clone.1 | custom fusion | flops 4194304 | bytes 25165824 | tf_op jit(solution)/shard_map/while/body/eval_jaxpr/scatter-add | solution.py:63
  394.0 9.4 %broadcast_multiply_fusion.3 = f32[1024,32,128]{2,1,0:T(8,128)} fusion(f32[1024,32]{1,0:T(8,128)S(1)} %dynamic-slice_bitcast_fusion.5, f32[1024,128]{1,0:T(8,128)S(1)} %bitcast_convert_fusion.2), kind=kLoop, calls=%fused_computation.5.clone.1 | loop fusion | flops 4194304 | bytes 17432576 | tf_op jit(solution)/shard_map/while/body/eval_jaxpr/mul | solution.py:60
  403.4 44.0 %scatter_custom_fusion.5 = f32[512,4096]{1,0:T(8,128)} fusion(f32[512,4096]{1,0:T(8,128)} %get-tuple-element.192, s32[1024]{0:T(1024)S(1)} %bitcast.86, f32[128,8,32,128]{3,2,1,0:T(8,128)} %bitcast.75), kind=kCustom, calls=%fused_computation.2.clone.1 | custom fusion | flops 4194304 | bytes 25165824 | tf_op jit(solution)/shard_map/while/body/eval_jaxpr/scatter-add | solution.py:63
  447.5 9.4 %broadcast_multiply_fusion.3 = f32[1024,32,128]{2,1,0:T(8,128)} fusion(f32[1024,32]{1,0:T(8,128)S(1)} %dynamic-slice_bitcast_fusion.5, f32[1024,128]{1,0:T(8,128)S(1)} %bitcast_convert_fusion.2), kind=kLoop, calls=%fused_computation.5.clone.1 | loop fusion | flops 4194304 | bytes 17432576 | tf_op jit(solution)/shard_map/while/body/eval_jaxpr/mul | solution.py:60
  456.9 44.0 %scatter_custom_fusion.5 = f32[512,4096]{1,0:T(8,128)} fusion(f32[512,4096]{1,0:T(8,128)} %get-tuple-element.192, s32[1024]{0:T(1024)S(1)} %bitcast.86, f32[128,8,32,128]{3,2,1,0:T(8,128)} %bitcast.75), kind=kCustom, calls=%fused_computation.2.clone.1 | custom fusion | flops 4194304 | bytes 25165824 | tf_op jit(solution)/shard_map/while/body/eval_jaxpr/scatter-add | solution.py:63
  500.9 8.4 %copy.21 = f32[64,8,32,128]{3,2,1,0:T(8,128)} copy(f32[64,8,32,128]{3,1,2,0:T(8,128)} %bitcast.79) | data formatting | bytes 16777216
  509.4 85.0 %reduce-scatter.2.cloned.1.call-done = f32[8,4,32,128]{3,2,1,0:T(8,128)} async-done(((f32[128,4,32,128]{3,2,1,0:T(8,128)}), f32[8,4,32,128]{3,2,1,0:T(8,128)}) %reduce-scatter.2.cloned.1.call-update) | async-done | bytes 524304 | tf_op jit(solution)/shard_map/reduce_scatter | solution.py:115
  595.3 1.2 fusion.16
  (63 shorter events, 12.9 us)
Async XLA Ops:
  7.2 1.0 copy-start
  7.2 67.1 %copy-start.1 = (bf16[1024,4,128]{2,1,0:T(4,128)(2,1)S(1)}, bf16[1024,4,128]{2,1,0:T(4,128)(2,1)}, u32[]{:S(2)}) copy-start(bf16[1024,4,128]{2,1,0:T(4,128)(2,1)} %param.16) | copy-start | bytes 3145732
  7.2 58.8 %all-gather.2.cloned.1.call-start = ((), (), s32[]{:S(2)}) async-start(), calls=%async_computation.1 | async-start | bytes 4456448 | tf_op jit(solution)/shard_map/all_gather | solution.py:94
  10.9 270.2 %all-reduce.2.cloned.1.call-start = ((), (), s32[]{:S(2)}) async-start(), calls=%async_computation.2 | async-start | bytes 1048576 | tf_op jit(solution)/shard_map/psum | solution.py:78
  74.2 148.4 %copy-start.3 = (f32[1024]{0:T(1024)S(1)}, f32[1024]{0:T(1024)}, u32[]{:S(2)}) copy-start(f32[1024]{0:T(1024)} %param.17) | copy-start | bytes 12292
  222.6 371.8 %reduce-scatter.2.cloned.1.call-start = ((), (), s32[]{:S(2)}) async-start(), calls=%async_computation.3 | async-start | bytes 8912896 | tf_op jit(solution)/shard_map/reduce_scatter | solution.py:115
  509.3 86.0 %copy-start.4 = (f32[8]{0:T(128)S(1)}, f32[8]{0:T(128)}, u32[]{:S(2)}) copy-start(f32[8]{0:T(128)} %param.13) | copy-start | bytes 100
  509.4 87.2 %copy-start.2 = (bf16[8,4,32,128]{3,2,1,0:T(8,128)(2,1)S(1)}, bf16[8,4,32,128]{3,2,1,0:T(8,128)(2,1)}, u32[]{:S(2)}) copy-start(bf16[8,4,32,128]{3,2,1,0:T(8,128)(2,1)} %param.11) | copy-start | bytes 786436
Sparse Core Ops, SparseCore 0:
  11.0 54.8 all-gather.1
  222.7 58.3 all-reduce.1
  509.5 84.8 reduce-scatter.1
where the time goes:
time: 606 us; the launch traced here: 605 us
  other arithmetic  226 us (37%)
  waiting for transfers between devices  196 us (32%)
  local copies, waits for them, and re-layouts  135 us (22%)
  matrix products  33.4 us (6%)
  between operations  13.9 us (2%)
    scatter-add x4, other arithmetic, accumulate(): return (summed_total.at[rows_here].add(contrib, mode='drop'), None)  176 us
    reduce_scatter x1, waiting for transfers between devices, per_device(): lax.psum_scatter(adjoint_terms, 'snd', scatter_dimension=0, tiled=True)  85 us
    gather x4, local copies, waits for them, and re-layouts, forward(): fetched = lookup[rows_here].reshape(block_rows, probe_count, cell_count)  71.2 us
    psum x1, waiting for transfers between devices, weigh(): seen_sums = lax.psum(partial_value, 'cell')  58.4 us
    all_gather x1, waiting for transfers between devices, per_device(): gathered = lax.all_gather(prior_field, 'snd', axis=0, tiled=True)  52.4 us
    while x4, local copies, waits for them, and re-layouts  37.8 us
    mul x4, other arithmetic, accumulate(): shape_here.astype(jnp.float32)[:, None, :] * values_here[:, :, None]  37.5 us
    dot_general x4, matrix products, forward(): jnp.einsum('epc,ec->ep', fetched, shape_here, preferred_element_type=jnp....  31.1 us
  transfers between devices with their start and end apart: 3, of which 3 were waited for; matrix products, arithmetic and copies ran while one was open for 0% of the time, Pallas kernels for 0%

commit v1 on v0

v1 whole, which is shorter than its diff:
```python
import functools

import jax
import jax.numpy as jnp
from jax import lax
from jax.experimental import pallas as pl
from jax.experimental.pallas import tpu as pltpu
from jax.sharding import PartitionSpec as P

BF = jnp.bfloat16
F32 = jnp.float32
MESH = pl.DeviceIdType.MESH

TT = 8
SLOTS = 64
WEEKS = 4
PROBES = 32
CELLS = 128


def dot_nn(a, b):
    return lax.dot_general(a, b, (((1,), (0,)), ((), ())), preferred_element_type=F32)


def dot_nt(a, b):
    return lax.dot_general(a, b, (((1,), (1,)), ((), ())), preferred_element_type=F32)


def iota(shape, dim):
    return lax.broadcasted_iota(jnp.int32, shape, dim)


def low_half(rows):
    return iota((rows, 128), 1) < 64


def pack(block, odd):
    low = low_half(16)
    if odd:
        return jnp.where(low, pltpu.roll(block[:16], 64, 1), block[16:])
    return jnp.where(low, block[:16], pltpu.roll(block[16:], 64, 1))


def unpack(even, odd):
    low = low_half(16)
    upper = jnp.where(low, even, pltpu.roll(odd, 64, 1))
    lower = jnp.where(low, pltpu.roll(even, 64, 1), odd)
    return jnp.concatenate([upper, lower], axis=0)


def doubled(ranks):
    rows, cols = ranks.shape
    wide = ranks.reshape(rows // 8, 8, cols)
    return jnp.concatenate([wide, wide - 1.0], axis=1).reshape(2 * rows, cols).astype(BF)


def one_hot(ranks):
    rows, cols = ranks.shape
    wide = ranks.reshape(rows // 16, 16, cols)
    one, zero = jnp.ones((), BF), jnp.zeros((), BF)
    rows_of = [jnp.where(wide == jnp.asarray(2 * q, BF), one, zero) for q in range(4)]
    return jnp.concatenate(rows_of, axis=1).reshape(4 * rows, cols)


def kernel(
    ns, nc, sound,
    probes_ref, spatial_ref, rho_ref, tile_ref, week_ref, foot_hbm, sigma_ref,
    image_ref, drop_ref,
    foot_ref, ranks_ref, hot_ref, field_ref,
    send_f, recv_f, send_k, recv_k, send_v, recv_v, send_r, recv_r, send_w, recv_w, send_p, recv_p,
    load_sem, ss_f, rs_f, ss_k, rs_k, ss_v, rs_v, ss_r, rs_r, ss_w, rs_w, ss_p, rs_p,
):
    me = lax.axis_index("snd")
    mine = lax.axis_index("cell")
    nj = ns * TT
    blocks = sound // 128
    chunk = sound // nc

    load = pltpu.make_async_copy(foot_hbm, foot_ref, load_sem)
    load.start()

    barrier = pltpu.get_barrier_semaphore()

    @pl.loop(1, ns)
    def _(d):
        pl.semaphore_signal(barrier, inc=1, device_id={"snd": (me + d) % ns, "cell": mine}, device_id_type=MESH)

    @pl.loop(1, nc)
    def _(d):
        pl.semaphore_signal(barrier, inc=1, device_id={"snd": me, "cell": (mine + d) % nc}, device_id_type=MESH)

    def to_snd(src, dst, ss, rs, dest):
        return pltpu.make_async_remote_copy(
            src_ref=src.at[dest], dst_ref=dst.at[me], send_sem=ss.at[dest], recv_sem=rs.at[me],
            device_id={"snd": dest, "cell": mine}, device_id_type=MESH,
        )

    def from_snd(src, dst, ss, rs, source):
        return pltpu.make_async_remote_copy(
            src_ref=src.at[source], dst_ref=dst.at[source], send_sem=ss.at[source], recv_sem=rs.at[source],
            device_id={"snd": source, "cell": mine}, device_id_type=MESH,
        )

    def to_cell(src, dst, ss, rs, dest):
        return pltpu.make_async_remote_copy(
            src_ref=src, dst_ref=dst.at[mine], send_sem=ss.at[dest], recv_sem=rs.at[mine],
            device_id={"snd": me, "cell": dest}, device_id_type=MESH,
        )

    def from_cell(src, dst, ss, rs, source):
        return pltpu.make_async_remote_copy(
            src_ref=src, dst_ref=dst.at[source], send_sem=ss.at[source], recv_sem=rs.at[source],
            device_id={"snd": me, "cell": source}, device_id_type=MESH,
        )

    def send_all(src, dst, ss, rs):
        dst[me] = src[me]

        @pl.loop(1, ns)
        def _(d):
            to_snd(src, dst, ss, rs, (me + d) % ns).start()

    def wait_all(src, dst, ss, rs):
        @pl.loop(1, ns)
        def _(d):
            from_snd(src, dst, ss, rs, (me + d) % ns).wait_recv()

    tiles = tile_ref[...]
    shift = nc.bit_length() - 1
    matched = ((tiles >> 3) & (nc - 1)) == mine
    local = jnp.where(matched, ((tiles >> (3 + shift)) << 3) | (tiles & 7), -1)
    weeks = week_ref[...]
    row_j = iota((nj, 256), 0)
    upper = jnp.where(iota((256, 256), 0) < iota((256, 256), 1), 1.0, 0.0).astype(BF)
    counts = jnp.concatenate([upper, jnp.ones((256, 256), BF)], axis=1)
    spread_e = jnp.where(iota((128, 512), 0) == iota((128, 512), 1) >> 2, 1.0, 0.0).astype(BF)
    pick_k = (iota((WEEKS, 512), 1) & 3) == iota((WEEKS, 512), 0)
    row_e = iota((nj, 512), 0).astype(F32)
    carry = jnp.zeros((nj, 256), F32)
    ranks_n = []
    weeks_n = []
    for b in range(sound // 256):
        lanes = slice(256 * b, 256 * b + 256)
        named = jnp.zeros((nj, 256), F32)
        week_of = jnp.zeros((nj, 256), F32)
        for k in range(4):
            same = local[k : k + 1, lanes] == row_j
            named = jnp.where(same, 1.0, named)
            week_of = jnp.where(same, weeks[k : k + 1, lanes].astype(F32), week_of)
        counted = dot_nn(named.astype(BF), counts)
        rank = jnp.where(named > 0.0, counted[:, :256] + carry, -1.0)
        carry = carry + counted[:, 256:]
        ranks_n.append(rank)
        weeks_n.append(week_of.astype(BF))
        for half in range(2):
            a = 2 * b + half
            here = slice(128 * a, 128 * a + 128)
            spread_rank = dot_nn(rank[:, 128 * half : 128 * half + 128].astype(BF), spread_e)
            spread_tile = dot_nn(local[:, here].astype(F32).astype(BF), spread_e)
            tile_e = jnp.sum(jnp.where(pick_k, spread_tile, 0.0), axis=0, keepdims=True)
            ranks_ref[a] = doubled(jnp.where(tile_e == row_e, spread_rank, -1.0))

    pl.semaphore_wait(barrier, ns - 1 + nc - 1)
    load.wait()

    groups = ns // 4
    mx, mz = me // 4, me % 4
    for g in range(groups):
        gx = (mx + 1 + g) % groups
        rows = pl.ds(pl.multiple_of(gx * 64, 64), 64)
        total = jnp.zeros((256, CELLS), F32)
        for a in range(blocks):
            total = total + dot_nn(one_hot(ranks_ref[a, rows, :]), foot_ref[512 * a : 512 * a + 512, :])
        send_f[pl.ds(pl.multiple_of(gx * 4, 4), 4)] = total.astype(BF).reshape(4, SLOTS, CELLS)
        if g < groups - 1:
            for dz in range(4):
                to_snd(send_f, recv_f, ss_f, rs_f, gx * 4 + (mz + dz) % 4).start()
        else:
            for dz in range(1, 4):
                to_snd(send_f, recv_f, ss_f, rs_f, gx * 4 + (mz + dz) % 4).start()
    recv_f[me] = send_f[me]

    for b in range(sound // 256):
        hot_ref[:, 256 * b : 256 * b + 256] = one_hot(doubled(ranks_n[b]))
    week_nj = jnp.concatenate(weeks_n, axis=1)
    half_tile = (iota((16, 128), 1) & 7) == (iota((16, 128), 0) & 7)
    half_own = (iota((16, 128), 1) < 64) == (iota((16, 128), 0) < 8)
    for b in range(ns // 2):
        found = dot_nt(week_nj[16 * b : 16 * b + 16], hot_ref[128 * b : 128 * b + 128, :])
        found = jnp.where(half_tile & half_own, found, 0.0)
        found = found + pltpu.roll(found, 64, 1)
        for odd in range(2):
            row = jnp.sum(found[8 * odd : 8 * odd + 8], axis=0, keepdims=True)
            send_k[2 * b + odd] = jnp.broadcast_to(row, (16, 128)).astype(BF)
    send_all(send_k, recv_k, ss_k, rs_k)

    for t in range(TT):
        spread = dot_nt(probes_ref[t], spatial_ref[t])
        running = spread[:PROBES]
        field_ref[t, :PROBES] = running.astype(BF)
        for w in range(1, WEEKS):
            running = spread[PROBES * w : PROBES * w + PROBES] + rho_ref[t] * running
            field_ref[t, PROBES * w : PROBES * w + PROBES] = running.astype(BF)

    wait_all(send_f, recv_f, ss_f, rs_f)
    wait_all(send_k, recv_k, ss_k, rs_k)
    lane_tile = iota((PROBES, 128), 1) & 7
    fields = field_ref[...].reshape(TT * WEEKS * PROBES, CELLS)
    codes = []
    for b in range(ns // 2):
        code = jnp.where(low_half(16), recv_k[2 * b].astype(F32), recv_k[2 * b + 1].astype(F32))
        codes.append(jnp.concatenate([code, code], axis=0))
    for b in range(ns // 2):
        full = dot_nt(fields, recv_f[2 * b : 2 * b + 2].reshape(128, CELLS))
        full = full.reshape(TT, WEEKS, PROBES, 128)
        value = jnp.zeros((PROBES, 128), F32)
        for w in range(WEEKS):
            here = full[0, w]
            for t in range(1, TT):
                here = jnp.where(lane_tile == t, full[t, w], here)
            value = jnp.where(codes[b] == float(w), here, value)
        for odd in range(2):
            send_v[2 * b + odd] = pack(value, odd).astype(BF)
    send_all(send_v, recv_v, ss_v, rs_v)
    wait_all(send_v, recv_v, ss_v, rs_v)

    values = jnp.concatenate(
        [unpack(recv_v[2 * b].astype(F32), recv_v[2 * b + 1].astype(F32)).astype(BF) for b in range(ns // 2)], axis=1
    )
    seen = dot_nn(values, hot_ref[...])
    for c in range(nc):
        send_r[c] = seen[:, chunk * c : chunk * c + chunk]

    @pl.loop(1, nc)
    def _(d):
        dest = (mine + d) % nc
        to_cell(send_r.at[dest], recv_r, ss_r, rs_r, dest).start()

    recv_r[mine] = send_r[mine]

    @pl.loop(1, nc)
    def _(d):
        source = (mine + d) % nc
        from_cell(send_r.at[source], recv_r, ss_r, rs_r, source).wait_recv()

    total = recv_r[0]
    for c in range(1, nc):
        total = total + recv_r[c]
    sigma = sigma_ref[pl.ds(mine, 1), :]
    send_w[...] = (total / (sigma * sigma)).astype(BF)

    @pl.loop(1, nc)
    def _(d):
        to_cell(send_w, recv_w, ss_w, rs_w, (mine + d) % nc).start()

    recv_w[mine] = send_w[...]

    @pl.loop(1, nc)
    def _(d):
        from_cell(send_w, recv_w, ss_w, rs_w, (mine + d) % nc).wait_recv()

    weighted = jnp.concatenate([recv_w[c] for c in range(nc)], axis=1)
    slot_values = dot_nt(weighted, hot_ref[...])
    for b in range(ns // 2):
        for odd in range(2):
            send_p[2 * b + odd] = pack(slot_values[:, 128 * b : 128 * b + 128], odd).astype(BF)
    send_all(send_p, recv_p, ss_p, rs_p)
    wait_all(send_p, recv_p, ss_p, rs_p)

    slot_weights = [unpack(recv_p[2 * b].astype(F32), recv_p[2 * b + 1].astype(F32)) for b in range(ns // 2)]
    feet = recv_f[...].reshape(ns * SLOTS, CELLS)
    for t in range(TT):
        parts = []
        for b in range(ns // 2):
            kept = jnp.where(lane_tile == t, slot_weights[b], 0.0)
            by_week = [jnp.where(codes[b] == float(w), kept, 0.0) for w in range(WEEKS)]
            parts.append(jnp.concatenate(by_week, axis=0).astype(BF))
        adjoint = dot_nn(jnp.concatenate(parts, axis=1), feet)
        running = adjoint[PROBES * (WEEKS - 1) :]
        carried = [running]
        for w in range(WEEKS - 2, -1, -1):
            running = adjoint[PROBES * w : PROBES * w + PROBES] + rho_ref[t] * running
            carried.append(running)
        image = dot_nn(jnp.concatenate(carried[::-1], axis=0).astype(BF), spatial_ref[t])
        image_ref[t] = image
        product = (probes_ref[t].astype(F32) * image).reshape(WEEKS, PROBES, CELLS)
        drop_ref[t] = jnp.sum(product, axis=1) * (1.0 / PROBES)

    @pl.loop(1, ns)
    def _(d):
        other = (me + d) % ns
        from_snd(send_f, recv_f, ss_f, rs_f, other).wait_send()
        from_snd(send_k, recv_k, ss_k, rs_k, other).wait_send()
        from_snd(send_v, recv_v, ss_v, rs_v, other).wait_send()
        from_snd(send_p, recv_p, ss_p, rs_p, other).wait_send()

    @pl.loop(1, nc)
    def _(d):
        other = (mine + d) % nc
        from_cell(send_r.at[other], recv_r, ss_r, rs_r, other).wait_send()
        from_cell(send_w, recv_w, ss_w, rs_w, other).wait_send()


def per_device(probes, spatial, rho, foot_tile, foot_week, footprint, sigma):
    ns, nc = lax.axis_size("snd"), lax.axis_size("cell")
    sound = foot_tile.shape[0]
    chunk = sound // nc
    vmem = pl.BlockSpec(memory_space=pltpu.VMEM)
    dma = lambda n: pltpu.SemaphoreType.DMA((n,))
    image, drop = pl.pallas_call(
        functools.partial(kernel, ns, nc, sound),
        out_shape=(
            jax.ShapeDtypeStruct((TT, WEEKS * PROBES, CELLS), F32),
            jax.ShapeDtypeStruct((TT, WEEKS, CELLS), F32),
        ),
        in_specs=[vmem, vmem, pl.BlockSpec(memory_space=pltpu.SMEM), vmem, vmem, pl.BlockSpec(memory_space=pl.ANY), vmem],
        out_specs=(vmem, vmem),
        scratch_shapes=[
            pltpu.VMEM((sound * 4, CELLS), BF),
            pltpu.VMEM((sound // 128, ns * 16, 512), BF),
            pltpu.VMEM((ns * SLOTS, sound), BF),
            pltpu.VMEM((TT, WEEKS * PROBES, CELLS), BF),
            pltpu.VMEM((ns, SLOTS, CELLS), BF),
            pltpu.VMEM((ns, SLOTS, CELLS), BF),
            pltpu.VMEM((ns, 16, 128), BF),
            pltpu.VMEM((ns, 16, 128), BF),
            pltpu.VMEM((ns, 16, 128), BF),
            pltpu.VMEM((ns, 16, 128), BF),
            pltpu.VMEM((nc, PROBES, chunk), F32),
            pltpu.VMEM((nc, PROBES, chunk), F32),
            pltpu.VMEM((PROBES, chunk), BF),
            pltpu.VMEM((nc, PROBES, chunk), BF),
            pltpu.VMEM((ns, 16, 128), BF),
            pltpu.VMEM((ns, 16, 128), BF),
            pltpu.SemaphoreType.DMA,
            dma(ns), dma(ns), dma(ns), dma(ns), dma(ns), dma(ns),
            dma(nc), dma(nc), dma(nc), dma(nc), dma(ns), dma(ns),
        ],
        compiler_params=pltpu.CompilerParams(
            collective_id=0, has_side_effects=True, vmem_limit_bytes=48 * 1024 * 1024
        ),
    )(
        probes.reshape(TT, WEEKS * PROBES, CELLS),
        spatial,
        rho,
        foot_tile.T,
        foot_week.T,
        footprint.reshape(sound * 4, CELLS),
        sigma.reshape(nc, chunk),
    )
    return image.reshape(TT, WEEKS, PROBES, CELLS), drop


def solution(mesh):
    placed = (
        P(("snd", "cell"), None, None, None),
        P(("snd", "cell"), None, None),
        P(("snd", "cell")),
        P("snd", None),
        P("snd", None),
        P("snd", None, None),
        P("snd"),
    )
    return jax.shard_map(
        per_device,
        mesh=mesh,
        in_specs=placed,
        out_specs=(P(("snd", "cell"), None, None, None), P(("snd", "cell"), None, None)),
        check_vma=False,
    )
```

time: 606 us -> 46.8 us (0.08)
  other arithmetic: 226 us -> 0 us
  waiting for transfers between devices: 196 us -> 0 us
  local copies, waits for them, and re-layouts: 135 us -> 6.63 us
  Pallas kernels: 0 us -> 39.2 us
  matrix products: 33.4 us -> 0 us
  between operations: 13.9 us -> 0.66 us
    scatter-add x4 -> x0, other arithmetic: 176 us -> none  [accumulate(): return (summed_total.at[rows_here].add(contrib, mode='drop'), None)]
    reduce_scatter x1 -> x0, waiting for transfers between devices: 85 us -> none  [per_device(): lax.psum_scatter(adjoint_terms, 'snd', scatter_dimension=0, tiled=True)]
    gather x4 -> x0, local copies, waits for them, and re-layouts: 71.2 us -> none  [forward(): fetched = lookup[rows_here].reshape(block_rows, probe_count, cell_count)]
    psum x1 -> x0, waiting for transfers between devices: 58.4 us -> none  [weigh(): seen_sums = lax.psum(partial_value, 'cell')]
    all_gather x1 -> x0, waiting for transfers between devices: 52.4 us -> none  [per_device(): gathered = lax.all_gather(prior_field, 'snd', axis=0, tiled=True)]
    pallas_call x0 -> x1, Pallas kernels: none -> 39.2 us  [per_device(): pl.pallas_call(functools.partial(kernel, ns, nc, sound), out_shape=(jax.S...]
    while x4 -> x0, local copies, waits for them, and re-layouts: 37.8 us -> none
    mul x5 -> x0, other arithmetic: 37.5 us -> none  [the longest x4 37.5 us: accumulate(): shape_here.astype(jnp.float32)[:, None, :] * values_here[:, :, None]]
  transfers between devices with their start and end apart: 3 -> 0, of which waited for: 3 -> 0; matrix products, arithmetic and copies ran while one was open for 0% -> 0% of each run, Pallas kernels for 0% -> 0%
where the time goes in v1:
time: 46.8 us; the launch traced here: 46.5 us
  Pallas kernels  39.2 us (84%)
  local copies, waits for them, and re-layouts  6.63 us (14%)
  between operations  0.66 us (1%)
    pallas_call x1, Pallas kernels, per_device(): pl.pallas_call(functools.partial(kernel, ns, nc, sound), out_shape=(jax.S...  39.2 us
    unnamed x16, local copies, waits for them, and re-layouts  6.63 us

profile of v1, /device:TPU:1, one launch (start us, length us, event | category | flops | bytes accessed | tf_op | source)
XLA Modules:
  0.0 46.5 jit_solution(11874030341273791067)
XLA Ops:
  0.6 0.0 copy-start.5
  0.6 0.0 copy-start.6
  0.7 0.7 %copy-done.5 = f32[1024]{0:T(1024)S(1)} copy-done((f32[1024]{0:T(1024)S(1)}, f32[1024]{0:T(1024)}, u32[]{:S(2)}) %copy-start.5) | copy-done | bytes 4120
  1.3 0.0 copy-done.6
  1.3 0.0 copy-start
  1.3 1.2 %copy-done = bf16[1024,4,128]{2,1,0:T(4,128)(2,1)S(1)} copy-done((bf16[1024,4,128]{2,1,0:T(4,128)(2,1)S(1)}, bf16[1024,4,128]{2,1,0:T(4,128)(2,1)}, u32[]{:S(2)}) %copy-start) | copy-done | bytes 1048600
  2.5 0.0 copy-start.1
  2.6 0.9 %copy-done.1 = bf16[8,4,32,128]{3,2,1,0:T(8,128)(2,1)S(1)} copy-done((bf16[8,4,32,128]{3,2,1,0:T(8,128)(2,1)S(1)}, bf16[8,4,32,128]{3,2,1,0:T(8,128)(2,1)}, u32[]{:S(2)}) %copy-start.1) | copy-done | bytes 262168
  3.5 0.0 copy-start.2
  3.5 0.9 %copy-done.2 = bf16[8,128,128]{2,1,0:T(8,128)(2,1)S(1)} copy-done((bf16[8,128,128]{2,1,0:T(8,128)(2,1)S(1)}, bf16[8,128,128]{2,1,0:T(8,128)(2,1)}, u32[]{:S(2)}) %copy-start.2) | copy-done | bytes 262168
  4.4 0.0 copy-start.3
  4.5 0.7 %copy-done.3 = s32[1024,4]{0,1:T(4,128)S(1)} copy-done((s32[1024,4]{0,1:T(4,128)S(1)}, s32[1024,4]{0,1:T(4,128)}, u32[]{:S(2)}) %copy-start.3) | copy-done | bytes 16408
  5.2 0.0 copy-start.4
  5.2 0.7 %copy-done.4 = s32[1024,4]{0,1:T(4,128)S(1)} copy-done((s32[1024,4]{0,1:T(4,128)S(1)}, s32[1024,4]{0,1:T(4,128)}, u32[]{:S(2)}) %copy-start.4) | copy-done | bytes 16408
  5.9 39.2 %shard_map.86 = (f32[8,128,128]{2,1,0:T(8,128)S(1)}, f32[8,4,128]{2,1,0:T(4,128)S(1)}) custom-call(bf16[8,128,128]{2,1,0:T(8,128)(2,1)S(1)} %bitcast.8, bf16[8,128,128]{2,1,0:T(8,128)(2,1)S(1)} %copy-done.2, f32[8]{0:T(128)S(1)} %copy-done.6, s32[4,1024]{1,0:T(4,128)S(1)} %bitcast.9, s32[4,1024]{1,0:T(4,128)S(1)} %bitcast.10, bf16[4096,128]{1,0:T(8,128)(2,1)S(1)} %bitcast.6, ...), custom_call_target="tpu_custom_call" | custom-call | tf_op jit(solution)/shard_map/pallas_call | solution.py:310
  45.1 0.8 %copy.11 = f32[8,4,32,128]{3,2,1,0:T(8,128)} copy(f32[8,4,32,128]{3,2,1,0:T(8,128)S(1)} %bitcast.7) | data formatting | bytes 1048576
  45.9 0.6 %copy.12 = f32[8,4,128]{2,1,0:T(4,128)} copy(f32[8,4,128]{2,1,0:T(4,128)S(1)} %get-tuple-element.9) | data formatting | bytes 32768
Async XLA Ops:
  0.6 0.7 %copy-start.5 = (f32[1024]{0:T(1024)S(1)}, f32[1024]{0:T(1024)}, u32[]{:S(2)}) copy-start(f32[1024]{0:T(1024)} %param.13) | copy-start | bytes 12292
  0.6 0.7 %copy-start.6 = (f32[8]{0:T(128)S(1)}, f32[8]{0:T(128)}, u32[]{:S(2)}) copy-start(f32[8]{0:T(128)} %rho_ref.1) | copy-start | bytes 100
  1.3 1.2 %copy-start = (bf16[1024,4,128]{2,1,0:T(4,128)(2,1)S(1)}, bf16[1024,4,128]{2,1,0:T(4,128)(2,1)}, u32[]{:S(2)}) copy-start(bf16[1024,4,128]{2,1,0:T(4,128)(2,1)} %param.12) | copy-start | bytes 3145732
  2.5 0.9 %copy-start.1 = (bf16[8,4,32,128]{3,2,1,0:T(8,128)(2,1)S(1)}, bf16[8,4,32,128]{3,2,1,0:T(8,128)(2,1)}, u32[]{:S(2)}) copy-start(bf16[8,4,32,128]{3,2,1,0:T(8,128)(2,1)} %param.7) | copy-start | bytes 786436
  3.5 0.9 %copy-start.2 = (bf16[8,128,128]{2,1,0:T(8,128)(2,1)S(1)}, bf16[8,128,128]{2,1,0:T(8,128)(2,1)}, u32[]{:S(2)}) copy-start(bf16[8,128,128]{2,1,0:T(8,128)(2,1)} %spatial_ref.1) | copy-start | bytes 786436
  4.4 0.7 %copy-start.3 = (s32[1024,4]{0,1:T(4,128)S(1)}, s32[1024,4]{0,1:T(4,128)}, u32[]{:S(2)}) copy-start(s32[1024,4]{0,1:T(4,128)} %param.10) | copy-start | bytes 49156
  5.2 0.7 %copy-start.4 = (s32[1024,4]{0,1:T(4,128)S(1)}, s32[1024,4]{0,1:T(4,128)}, u32[]{:S(2)}) copy-start(s32[1024,4]{0,1:T(4,128)} %param.11) | copy-start | bytes 49156

commit v2 on v1

v2 whole, which is shorter than its diff:
```python
import functools

import jax
import jax.numpy as jnp
from jax import lax
from jax.experimental import pallas as pl
from jax.experimental.pallas import tpu as pltpu
from jax.sharding import PartitionSpec as P

BF = jnp.bfloat16
F32 = jnp.float32
MESH = pl.DeviceIdType.MESH

TT = 8
SLOTS = 64
WEEKS = 4
PROBES = 32
CELLS = 128


def dot_nn(a, b):
    return lax.dot_general(a, b, (((1,), (0,)), ((), ())), preferred_element_type=F32)


def dot_nt(a, b):
    return lax.dot_general(a, b, (((1,), (1,)), ((), ())), preferred_element_type=F32)


def iota(shape, dim):
    return lax.broadcasted_iota(jnp.int32, shape, dim)


def low_half(rows):
    return iota((rows, 128), 1) < 64


def packed(values):
    low = low_half(16)
    rows = []
    for lanes in (slice(0, 128), slice(128, 256)):
        upper, lower = values[:16, lanes], values[16:, lanes]
        rows.append(jnp.where(low, upper, pltpu.roll(lower, 64, 1)))
        rows.append(jnp.where(low, pltpu.roll(upper, 64, 1), lower))
    return jnp.stack(rows).astype(BF)


def unpacked(block):
    low = low_half(16)
    wide = block.astype(F32)
    cols = []
    for even, odd in ((wide[0], wide[1]), (wide[2], wide[3])):
        upper = jnp.where(low, even, pltpu.roll(odd, 64, 1))
        lower = jnp.where(low, pltpu.roll(even, 64, 1), odd)
        cols.append(jnp.concatenate([upper, lower], axis=0))
    return jnp.concatenate(cols, axis=1)


def doubled(ranks):
    rows, cols = ranks.shape
    wide = ranks.reshape(rows // 8, 8, cols)
    return jnp.concatenate([wide, wide - 1.0], axis=1).reshape(2 * rows, cols).astype(BF)


def one_hot(ranks):
    rows, cols = ranks.shape
    wide = ranks.reshape(rows // 16, 16, cols)
    one, zero = jnp.ones((), BF), jnp.zeros((), BF)
    rows_of = [jnp.where(wide == jnp.asarray(2 * q, BF), one, zero) for q in range(4)]
    return jnp.concatenate(rows_of, axis=1).reshape(4 * rows, cols)


def kernel(
    ns, nc, sound,
    probes_hbm, spatial_hbm, rho_hbm, tile_hbm, week_hbm, foot_hbm, sigma_hbm,
    image_ref, drop_ref,
    probes_ref, spatial_ref, rho_ref, tile_ref, week_ref, foot_ref, sigma_ref, ranks_ref, hot_ref, field_ref, adjoint_ref,
    send_f, recv_f, send_k, recv_k, send_v, recv_v, send_p, recv_p,
    send_c, recv_c, send_y, recv_y, recv_w,
    load_sem, ss_f, rs_f, ss_k, rs_k, ss_v, rs_v, ss_p, rs_p, ss_c, rs_c, ss_y, rs_y, ss_w, rs_w,
):
    me = lax.axis_index("snd")
    mine = lax.axis_index("cell")
    core, row_y = mine % 2, mine // 2
    nj = ns * TT
    groups = ns // 4
    ny = nc // 2
    half = sound // 2
    mx, mz = me // 4, me % 4
    near = {1: [0], 2: [0, 1], 4: [0, 1, 3, 2]}[groups]
    far = near[::-1]
    far_z = [2, 1, 3, 0]

    loads = [
        pltpu.make_async_copy(src, dst, load_sem.at[i])
        for i, (src, dst) in enumerate(
            (
                (tile_hbm, tile_ref),
                (week_hbm, week_ref),
                (foot_hbm, foot_ref),
                (spatial_hbm, spatial_ref),
                (probes_hbm, probes_ref),
                (sigma_hbm, sigma_ref),
                (rho_hbm, rho_ref),
            )
        )
    ]
    for load in loads:
        load.start()

    barrier = pltpu.get_barrier_semaphore()

    def greet(snd, cell):
        pl.semaphore_signal(barrier, inc=1, device_id={"snd": snd, "cell": cell}, device_id_type=MESH)

    def group_x(dx):
        return (mx + dx) % groups

    def partner(dx, dz):
        return group_x(dx) * 4 + (mz + dz) % 4

    for dx in far:
        for dz in far_z:
            if (dx, dz) != (0, 0):
                greet(partner(dx, dz), mine)
    for dy in range(1, ny):
        greet(me, (row_y + dy) % ny * 2 + core)
    greet(me, row_y * 2 + 1 - core)

    def over_snd(refs, there, here, other):
        src, dst, ss, rs = refs
        return pltpu.make_async_remote_copy(
            src_ref=src.at[there], dst_ref=dst.at[here], send_sem=ss.at[there], recv_sem=rs.at[here],
            device_id={"snd": other, "cell": mine}, device_id_type=MESH,
        )

    def to_snd(refs, dest):
        return over_snd(refs, dest, me, dest)

    def from_snd(refs, source):
        return over_snd(refs, source, source, source)

    of_f = (send_f, recv_f, ss_f, rs_f)
    of_k = (send_k, recv_k, ss_k, rs_k)
    of_v = (send_v, recv_v, ss_v, rs_v)
    of_p = (send_p, recv_p, ss_p, rs_p)

    def send_group(refs, dx):
        for dz in far_z:
            if (dx, dz) != (0, 0):
                to_snd(refs, partner(dx, dz)).start()
        if dx == 0:
            refs[1][me] = refs[0][me]

    def wait_group(refs, dx):
        for dz in range(4):
            if (dx, dz) != (0, 0):
                from_snd(refs, partner(dx, dz)).wait_recv()

    def group_rows(dx, size):
        return pl.ds(pl.multiple_of(group_x(dx) * 4 * size, 4 * size), 4 * size)

    def group_of(dx):
        return pl.ds(pl.multiple_of(group_x(dx) * 4, 4), 4)

    loads[0].wait()
    loads[1].wait()
    tiles = tile_ref[...]
    shift = nc.bit_length() - 1
    matched = ((tiles >> 3) & (nc - 1)) == mine
    local = jnp.where(matched, ((tiles >> (3 + shift)) << 3) | (tiles & 7), -1)
    weeks = week_ref[...]
    row_j = iota((nj, 256), 0)
    upper = jnp.where(iota((256, 256), 0) < iota((256, 256), 1), 1.0, 0.0).astype(BF)
    counts = jnp.concatenate([upper, jnp.ones((256, 256), BF)], axis=1)
    spread_e = jnp.where(iota((128, 512), 0) == iota((128, 512), 1) >> 2, 1.0, 0.0).astype(BF)
    pick_k = (iota((WEEKS, 512), 1) & 3) == iota((WEEKS, 512), 0)
    row_e = iota((nj, 512), 0).astype(F32)
    carry = jnp.zeros((nj, 256), F32)
    ranks_n = []
    weeks_n = []
    for b in range(sound // 256):
        lanes = slice(256 * b, 256 * b + 256)
        named = jnp.zeros((nj, 256), F32)
        week_of = jnp.zeros((nj, 256), F32)
        for k in range(4):
            same = local[k : k + 1, lanes] == row_j
            named = jnp.where(same, 1.0, named)
            week_of = jnp.where(same, weeks[k : k + 1, lanes].astype(F32), week_of)
        counted = dot_nn(named.astype(BF), counts)
        rank = jnp.where(named > 0.0, counted[:, :256] + carry, -1.0)
        carry = carry + counted[:, 256:]
        ranks_n.append(rank)
        weeks_n.append(week_of.astype(BF))
        for part in range(2):
            a = 2 * b + part
            here = slice(128 * a, 128 * a + 128)
            spread_rank = dot_nn(rank[:, 128 * part : 128 * part + 128].astype(BF), spread_e)
            spread_tile = dot_nn(local[:, here].astype(F32).astype(BF), spread_e)
            tile_e = jnp.sum(jnp.where(pick_k, spread_tile, 0.0), axis=0, keepdims=True)
            ranks_ref[a] = doubled(jnp.where(tile_e == row_e, spread_rank, -1.0))

    loads[2].wait()

    def pick_feet(dx):
        total = jnp.zeros((256, CELLS), F32)
        for a in range(sound // 128):
            total = total + dot_nn(one_hot(ranks_ref[a, group_rows(dx, 16), :]), foot_ref[512 * a : 512 * a + 512, :])
        send_f[group_of(dx)] = total.astype(BF).reshape(4, SLOTS, CELLS)

    for dx in far[:-1]:
        pick_feet(dx)
    if groups == 1:
        pick_feet(0)
    pl.semaphore_wait(barrier, ns - 1 + ny - 1 + 1)
    for dx in far[:-1]:
        send_group(of_f, dx)
    if groups > 1:
        pick_feet(0)
    send_group(of_f, 0)

    for b in range(sound // 256):
        hot_ref[:, 256 * b : 256 * b + 256] = one_hot(doubled(ranks_n[b]))
    week_nj = jnp.concatenate(weeks_n, axis=1)
    same_tile = (iota((16, 128), 1) & 7) == (iota((16, 128), 0) & 7)
    same_owner = (iota((16, 128), 1) < 64) == (iota((16, 128), 0) < 8)
    for b in range(ns // 2):
        found = dot_nt(week_nj[16 * b : 16 * b + 16], hot_ref[128 * b : 128 * b + 128, :])
        found = jnp.where(same_tile & same_owner, found, 0.0)
        found = found + pltpu.roll(found, 64, 1)
        for odd in range(2):
            row = jnp.sum(found[8 * odd : 8 * odd + 8], axis=0, keepdims=True)
            send_k[2 * b + odd] = jnp.broadcast_to(row, (16, 128)).astype(BF)
    for dx in far:
        send_group(of_k, dx)

    for load in loads[3:]:
        load.wait()
    for t in range(TT):
        spread = dot_nt(probes_ref[t], spatial_ref[t])
        running = spread[:PROBES]
        field_ref[t, :PROBES] = running.astype(BF)
        for w in range(1, WEEKS):
            running = spread[PROBES * w : PROBES * w + PROBES] + rho_ref[t] * running
            field_ref[t, PROBES * w : PROBES * w + PROBES] = running.astype(BF)

    lane_tile = iota((PROBES, 256), 1) & 7
    fields = field_ref[...].reshape(TT * WEEKS * PROBES, CELLS)
    codes = {}
    for dx in near:
        wait_group(of_f, dx)
        wait_group(of_k, dx)
        names = recv_k[group_of(dx)].astype(F32)
        low = low_half(16)
        code = jnp.concatenate([jnp.where(low, names[0], names[1]), jnp.where(low, names[2], names[3])], axis=1)
        codes[dx] = jnp.concatenate([code, code], axis=0)
        full = dot_nt(fields, recv_f[group_of(dx)].reshape(256, CELLS))
        full = full.reshape(TT, WEEKS, PROBES, 256)
        value = jnp.zeros((PROBES, 256), F32)
        for w in range(WEEKS):
            here = full[0, w]
            for t in range(1, TT):
                here = jnp.where(lane_tile == t, full[t, w], here)
            value = jnp.where(codes[dx] == float(w), here, value)
        send_v[group_of(dx)] = packed(value)
        send_group(of_v, dx)

    seen = jnp.zeros((PROBES, sound), F32)
    for dx in near:
        wait_group(of_v, dx)
        seen = seen + dot_nn(unpacked(recv_v[group_of(dx)]).astype(BF), hot_ref[group_rows(dx, SLOTS), :])
    send_c[0] = seen[:, :half]
    send_c[1] = seen[:, half:]
    other_core = {"snd": me, "cell": row_y * 2 + 1 - core}
    swap = pltpu.make_async_remote_copy(
        src_ref=send_c.at[1 - core], dst_ref=recv_c, send_sem=ss_c, recv_sem=rs_c,
        device_id=other_core, device_id_type=MESH,
    )
    swap.start()
    swap.wait_recv()
    total = send_c[core] + recv_c[...]
    send_y[...] = total.astype(BF)

    def over_y(dy, slot):
        return pltpu.make_async_remote_copy(
            src_ref=send_y, dst_ref=recv_y.at[slot], send_sem=ss_y.at[dy], recv_sem=rs_y.at[slot],
            device_id={"snd": me, "cell": (row_y + dy) % ny * 2 + core}, device_id_type=MESH,
        )

    steps_y = {1: [], 2: [1], 4: [2, 1, 3]}[ny]
    for dy in steps_y:
        over_y(dy, row_y).start()
    for dy in reversed(steps_y):
        over_y(dy, (row_y + dy) % ny).wait_recv()
        total = total + recv_y[(row_y + dy) % ny].astype(F32)
    own = half // 128
    sigma = jnp.concatenate([sigma_ref[pl.ds(core * own + i, 1), :] for i in range(own)], axis=1)
    recv_w[core] = (total / (sigma * sigma)).astype(BF)
    share = pltpu.make_async_remote_copy(
        src_ref=recv_w.at[core], dst_ref=recv_w.at[core], send_sem=ss_w, recv_sem=rs_w,
        device_id=other_core, device_id_type=MESH,
    )
    share.start()
    share.wait_recv()

    weighted = jnp.concatenate([recv_w[0], recv_w[1]], axis=1)
    for dx in far:
        send_p[group_of(dx)] = packed(dot_nt(weighted, hot_ref[group_rows(dx, SLOTS), :]))
        send_group(of_p, dx)

    for step, dx in enumerate(near):
        wait_group(of_p, dx)
        value = unpacked(recv_p[group_of(dx)])
        by_week = [jnp.where(codes[dx] == float(w), value, 0.0) for w in range(WEEKS)]
        spread = [jnp.where(lane_tile == t, by_week[w], 0.0).astype(BF) for t in range(TT) for w in range(WEEKS)]
        part = dot_nn(jnp.concatenate(spread, axis=0), recv_f[group_of(dx)].reshape(256, CELLS))
        if step == 0:
            adjoint_ref[...] = part
        else:
            adjoint_ref[...] += part
    for t in range(TT):
        rows = WEEKS * PROBES * t
        running = adjoint_ref[rows + PROBES * (WEEKS - 1) : rows + PROBES * WEEKS, :]
        carried = [running]
        for w in range(WEEKS - 2, -1, -1):
            running = adjoint_ref[rows + PROBES * w : rows + PROBES * w + PROBES, :] + rho_ref[t] * running
            carried.append(running)
        image = dot_nn(jnp.concatenate(carried[::-1], axis=0).astype(BF), spatial_ref[t])
        image_ref[t] = image
        product = (probes_ref[t].astype(F32) * image).reshape(WEEKS, PROBES, CELLS)
        drop_ref[t] = jnp.sum(product, axis=1) * (1.0 / PROBES)

    for refs in (of_f, of_k, of_v, of_p):
        for dx in far:
            for dz in far_z:
                if (dx, dz) != (0, 0):
                    to_snd(refs, partner(dx, dz)).wait_send()
    swap.wait_send()
    share.wait_send()
    for dy in steps_y:
        over_y(dy, row_y).wait_send()


def per_device(probes, spatial, rho, foot_tile, foot_week, footprint, sigma):
    ns, nc = lax.axis_size("snd"), lax.axis_size("cell")
    sound = foot_tile.shape[0]
    half = sound // 2
    hbm = pl.BlockSpec(memory_space=pltpu.HBM)
    vmem = pl.BlockSpec(memory_space=pltpu.VMEM)
    one = pltpu.SemaphoreType.DMA
    dma = lambda n: pltpu.SemaphoreType.DMA((n,))
    operands = (
        probes.reshape(TT, WEEKS * PROBES, CELLS),
        spatial,
        rho,
        foot_tile.T,
        foot_week.T,
        footprint.reshape(sound * 4, CELLS),
        sigma.reshape(sound // 128, 128),
    )
    image, drop = pl.pallas_call(
        functools.partial(kernel, ns, nc, sound),
        out_shape=(
            jax.ShapeDtypeStruct((TT, WEEKS * PROBES, CELLS), F32),
            jax.ShapeDtypeStruct((TT, WEEKS, CELLS), F32),
        ),
        in_specs=[hbm] * 7,
        out_specs=(vmem, vmem),
        scratch_shapes=[
            pltpu.VMEM((TT, WEEKS * PROBES, CELLS), BF),
            pltpu.VMEM((TT, CELLS, CELLS), BF),
            pltpu.SMEM((TT,), F32),
            pltpu.VMEM((4, sound), jnp.int32),
            pltpu.VMEM((4, sound), jnp.int32),
            pltpu.VMEM((sound * 4, CELLS), BF),
            pltpu.VMEM((sound // 128, 128), F32),
            pltpu.VMEM((sound // 128, ns * 16, 512), BF),
            pltpu.VMEM((ns * SLOTS, sound), BF),
            pltpu.VMEM((TT, WEEKS * PROBES, CELLS), BF),
            pltpu.VMEM((TT * WEEKS * PROBES, CELLS), F32),
            pltpu.VMEM((ns, SLOTS, CELLS), BF),
            pltpu.VMEM((ns, SLOTS, CELLS), BF),
            pltpu.VMEM((ns, 16, 128), BF),
            pltpu.VMEM((ns, 16, 128), BF),
            pltpu.VMEM((ns, 16, 128), BF),
            pltpu.VMEM((ns, 16, 128), BF),
            pltpu.VMEM((ns, 16, 128), BF),
            pltpu.VMEM((ns, 16, 128), BF),
            pltpu.VMEM((2, PROBES, half), F32),
            pltpu.VMEM((PROBES, half), F32),
            pltpu.VMEM((PROBES, half), BF),
            pltpu.VMEM((nc // 2, PROBES, half), BF),
            pltpu.VMEM((2, PROBES, half), BF),
            dma(7),
            dma(ns), dma(ns), dma(ns), dma(ns), dma(ns), dma(ns), dma(ns), dma(ns),
            one, one, dma(max(2, nc // 2)), dma(nc // 2), one, one,
        ],
        compiler_params=pltpu.CompilerParams(
            collective_id=0, has_side_effects=True, vmem_limit_bytes=40 * 1024 * 1024
        ),
    )(*(pltpu.with_memory_space_constraint(x, pltpu.HBM) for x in operands))
    return image.reshape(TT, WEEKS, PROBES, CELLS), drop


def solution(mesh):
    placed = (
        P(("snd", "cell"), None, None, None),
        P(("snd", "cell"), None, None),
        P(("snd", "cell")),
        P("snd", None),
        P("snd", None),
        P("snd", None, None),
        P("snd"),
    )
    return jax.shard_map(
        per_device,
        mesh=mesh,
        in_specs=placed,
        out_specs=(P(("snd", "cell"), None, None, None), P(("snd", "cell"), None, None)),
        check_vma=False,
    )
```

time: 46.8 us -> 38.4 us (0.82)
  local copies, waits for them, and re-layouts: 6.63 us -> 1.4 us
  Pallas kernels: 39.2 us -> 36.2 us
    unnamed x16 -> x2, local copies, waits for them, and re-layouts: 6.63 us -> 1.4 us
    pallas_call x1, Pallas kernels: 39.2 us -> 36.2 us  [per_device(): pl.pallas_call(functools.partial(kernel, ns, nc, sound), out_shape=(jax.S...]
where the time goes in v2:
time: 38.4 us; the launch traced here: 38.2 us
  Pallas kernels  36.2 us (94%)
  local copies, waits for them, and re-layouts  1.4 us (4%)
  between operations  0.64 us (2%)
    pallas_call x1, Pallas kernels, per_device(): pl.pallas_call(functools.partial(kernel, ns, nc, sound), out_shape=(jax.S...  36.2 us
    unnamed x2, local copies, waits for them, and re-layouts  1.4 us

profile of v2, /device:TPU:1, one launch (start us, length us, event | category | flops | bytes accessed | tf_op | source)
XLA Modules:
  0.0 38.2 jit_solution(1934913659518563633)
XLA Ops:
  0.6 36.2 %shard_map.86 = (f32[8,128,128]{2,1,0:T(8,128)S(1)}, f32[8,4,128]{2,1,0:T(4,128)S(1)}) custom-call(bf16[8,128,128]{2,1,0:T(8,128)(2,1)} %bitcast.8, bf16[8,128,128]{2,1,0:T(8,128)(2,1)} %spatial_hbm.1, f32[8]{0:T(128)} %rho_hbm.1, s32[4,1024]{1,0:T(4,128)} %bitcast.9, s32[4,1024]{1,0:T(4,128)} %bitcast.10, bf16[4096,128]{1,0:T(8,128)(2,1)} %bitcast.7, ...), custom_call_target="tpu_custom_call" | custom-call | tf_op jit(solution)/shard_map/pallas_call | solution.py:360
  36.8 0.8 %copy.11 = f32[8,4,32,128]{3,2,1,0:T(8,128)} copy(f32[8,4,32,128]{3,2,1,0:T(8,128)S(1)} %bitcast.6) | data formatting | bytes 1048576
  37.6 0.6 %copy.12 = f32[8,4,128]{2,1,0:T(4,128)} copy(f32[8,4,128]{2,1,0:T(4,128)S(1)} %get-tuple-element.9) | data formatting | bytes 32768

commit v3 on v2

--- a/solution.py
+++ b/solution.py
@@ -72,11 +72,11 @@
 def kernel(
     ns, nc, sound,
     probes_hbm, spatial_hbm, rho_hbm, tile_hbm, week_hbm, foot_hbm, sigma_hbm,
-    image_ref, drop_ref,
-    probes_ref, spatial_ref, rho_ref, tile_ref, week_ref, foot_ref, sigma_ref, ranks_ref, hot_ref, field_ref, adjoint_ref,
-    send_f, recv_f, send_k, recv_k, send_v, recv_v, send_p, recv_p,
+    carried_ref,
+    probes_ref, spatial_ref, rho_ref, tile_ref, week_ref, foot_ref, sigma_ref, order_ref, ranks_ref, hot_ref, field_ref, adjoint_ref,
+    send_f, recv_f, send_v, recv_v, send_p, recv_p,
     send_c, recv_c, send_y, recv_y, recv_w,
-    load_sem, ss_f, rs_f, ss_k, rs_k, ss_v, rs_v, ss_p, rs_p, ss_c, rs_c, ss_y, rs_y, ss_w, rs_w,
+    load_sem, ss_f, rs_f, ss_v, rs_v, ss_p, rs_p, ss_c, rs_c, ss_y, rs_y, ss_w, rs_w,
 ):
     me = lax.axis_index("snd")
     mine = lax.axis_index("cell")
@@ -140,7 +140,6 @@
         return over_snd(refs, source, source, source)
 
     of_f = (send_f, recv_f, ss_f, rs_f)
-    of_k = (send_k, recv_k, ss_k, rs_k)
     of_v = (send_v, recv_v, ss_v, rs_v)
     of_p = (send_p, recv_p, ss_p, rs_p)
 
@@ -165,39 +164,48 @@
     loads[0].wait()
     loads[1].wait()
     tiles = tile_ref[...]
+    weeks = week_ref[...]
     shift = nc.bit_length() - 1
-    matched = ((tiles >> 3) & (nc - 1)) == mine
-    local = jnp.where(matched, ((tiles >> (3 + shift)) << 3) | (tiles & 7), -1)
-    weeks = week_ref[...]
     row_j = iota((nj, 256), 0)
     upper = jnp.where(iota((256, 256), 0) < iota((256, 256), 1), 1.0, 0.0).astype(BF)
     counts = jnp.concatenate([upper, jnp.ones((256, 256), BF)], axis=1)
     spread_e = jnp.where(iota((128, 512), 0) == iota((128, 512), 1) >> 2, 1.0, 0.0).astype(BF)
     pick_k = (iota((WEEKS, 512), 1) & 3) == iota((WEEKS, 512), 0)
     row_e = iota((nj, 512), 0).astype(F32)
+
+    matched = ((tiles >> 3) & (nc - 1)) == mine
+    local = jnp.where(matched, ((tiles >> (3 + shift)) << 3) | (tiles & 7), -1)
     carry = jnp.zeros((nj, 256), F32)
-    ranks_n = []
-    weeks_n = []
+    bits = jnp.zeros((nj, 256), F32)
     for b in range(sound // 256):
         lanes = slice(256 * b, 256 * b + 256)
         named = jnp.zeros((nj, 256), F32)
-        week_of = jnp.zeros((nj, 256), F32)
+        week_of = jnp.zeros((nj, 256), jnp.int32)
         for k in range(4):
             same = local[k : k + 1, lanes] == row_j
             named = jnp.where(same, 1.0, named)
-            week_of = jnp.where(same, weeks[k : k + 1, lanes].astype(F32), week_of)
+            week_of = jnp.where(same, weeks[k : k + 1, lanes], week_of)
         counted = dot_nn(named.astype(BF), counts)
-        rank = jnp.where(named > 0.0, counted[:, :256] + carry, -1.0)
+        place = counted[:, :256] + carry
+        order = jnp.where(named > 0.0, place, -1.0)
         carry = carry + counted[:, 256:]
-        ranks_n.append(rank)
-        weeks_n.append(week_of.astype(BF))
+        bits = bits + (week_of << (place.astype(jnp.int32) * 2)).astype(F32)
+        order_ref[:, lanes] = order
         for part in range(2):
             a = 2 * b + part
             here = slice(128 * a, 128 * a + 128)
-            spread_rank = dot_nn(rank[:, 128 * part : 128 * part + 128].astype(BF), spread_e)
+            spread_rank = dot_nn(order[:, 128 * part : 128 * part + 128].astype(BF), spread_e)
             spread_tile = dot_nn(local[:, here].astype(F32).astype(BF), spread_e)
             tile_e = jnp.sum(jnp.where(pick_k, spread_tile, 0.0), axis=0, keepdims=True)
             ranks_ref[a] = doubled(jnp.where(tile_e == row_e, spread_rank, -1.0))
+
+    bits = jnp.sum(bits, axis=1, keepdims=True).astype(jnp.int32)
+    lane = iota((TT, 128), 1)
+    for d in range(ns):
+        word = jnp.broadcast_to(bits[TT * d : TT * d + TT], (TT, 128))
+        week = (word >> (((lane & 63) >> 3) * 2)) & 3
+        row = jnp.sum(jnp.where((lane & 7) == iota((TT, 128), 0), week.astype(F32), 0.0), axis=0, keepdims=True)
+        send_f[d, SLOTS:] = jnp.broadcast_to(row, (16, 128)).astype(BF)
 
     loads[2].wait()
 
@@ -205,7 +213,7 @@
         total = jnp.zeros((256, CELLS), F32)
         for a in range(sound // 128):
             total = total + dot_nn(one_hot(ranks_ref[a, group_rows(dx, 16), :]), foot_ref[512 * a : 512 * a + 512, :])
-        send_f[group_of(dx)] = total.astype(BF).reshape(4, SLOTS, CELLS)
+        send_f[group_of(dx), :SLOTS] = total.astype(BF).reshape(4, SLOTS, CELLS)
 
     for dx in far[:-1]:
         pick_feet(dx)
@@ -219,19 +227,8 @@
     send_group(of_f, 0)
 
     for b in range(sound // 256):
-        hot_ref[:, 256 * b : 256 * b + 256] = one_hot(doubled(ranks_n[b]))
-    week_nj = jnp.concatenate(weeks_n, axis=1)
-    same_tile = (iota((16, 128), 1) & 7) == (iota((16, 128), 0) & 7)
-    same_owner = (iota((16, 128), 1) < 64) == (iota((16, 128), 0) < 8)
-    for b in range(ns // 2):
-        found = dot_nt(week_nj[16 * b : 16 * b + 16], hot_ref[128 * b : 128 * b + 128, :])
-        found = jnp.where(same_tile & same_owner, found, 0.0)
-        found = found + pltpu.roll(found, 64, 1)
-        for odd in range(2):
-            row = jnp.sum(found[8 * odd : 8 * odd + 8], axis=0, keepdims=True)
-            send_k[2 * b + odd] = jnp.broadcast_to(row, (16, 128)).astype(BF)
-    for dx in far:
-        send_group(of_k, dx)
+        lanes = slice(256 * b, 256 * b + 256)
+        hot_ref[:, lanes] = one_hot(doubled(order_ref[:, lanes]))
 
     for load in loads[3:]:
         load.wait()
@@ -248,12 +245,11 @@
     codes = {}
     for dx in near:
         wait_group(of_f, dx)
-        wait_group(of_k, dx)
-        names = recv_k[group_of(dx)].astype(F32)
+        names = recv_f[group_of(dx), SLOTS:].astype(F32)
         low = low_half(16)
         code = jnp.concatenate([jnp.where(low, names[0], names[1]), jnp.where(low, names[2], names[3])], axis=1)
         codes[dx] = jnp.concatenate([code, code], axis=0)
-        full = dot_nt(fields, recv_f[group_of(dx)].reshape(256, CELLS))
+        full = dot_nt(fields, recv_f[group_of(dx), :SLOTS].reshape(256, CELLS))
         full = full.reshape(TT, WEEKS, PROBES, 256)
         value = jnp.zeros((PROBES, 256), F32)
         for w in range(WEEKS):
@@ -312,24 +308,21 @@
         value = unpacked(recv_p[group_of(dx)])
         by_week = [jnp.where(codes[dx] == float(w), value, 0.0) for w in range(WEEKS)]
         spread = [jnp.where(lane_tile == t, by_week[w], 0.0).astype(BF) for t in range(TT) for w in range(WEEKS)]
-        part = dot_nn(jnp.concatenate(spread, axis=0), recv_f[group_of(dx)].reshape(256, CELLS))
-        if step == 0:
-            adjoint_ref[...] = part
-        else:
-            adjoint_ref[...] += part
+        adjoint = dot_nn(jnp.concatenate(spread, axis=0), recv_f[group_of(dx), :SLOTS].reshape(256, CELLS))
+        if step > 0:
+            adjoint = adjoint + adjoint_ref[...]
+        if step < groups - 1:
+            adjoint_ref[...] = adjoint
     for t in range(TT):
         rows = WEEKS * PROBES * t
-        running = adjoint_ref[rows + PROBES * (WEEKS - 1) : rows + PROBES * WEEKS, :]
+        running = adjoint[rows + PROBES * (WEEKS - 1) : rows + PROBES * WEEKS]
         carried = [running]
         for w in range(WEEKS - 2, -1, -1):
-            running = adjoint_ref[rows + PROBES * w : rows + PROBES * w + PROBES, :] + rho_ref[t] * running
+            running = adjoint[rows + PROBES * w : rows + PROBES * w + PROBES] + rho_ref[t] * running
             carried.append(running)
-        image = dot_nn(jnp.concatenate(carried[::-1], axis=0).astype(BF), spatial_ref[t])
-        image_ref[t] = image
-        product = (probes_ref[t].astype(F32) * image).reshape(WEEKS, PROBES, CELLS)
-        drop_ref[t] = jnp.sum(product, axis=1) * (1.0 / PROBES)
-
-    for refs in (of_f, of_k, of_v, of_p):
+        carried_ref[t] = jnp.concatenate(carried[::-1], axis=0).astype(BF)
+
+    for refs in (of_f, of_v, of_p):
         for dx in far:
             for dz in far_z:
                 if (dx, dz) != (0, 0):
@@ -338,6 +331,21 @@
     share.wait_send()
     for dy in steps_y:
         over_y(dy, row_y).wait_send()
+
+
+def finish(carried_ref, spatial_ref, probes_ref, image_hbm, drop_hbm, image_ref, drop_ref, sems):
+    stores = [pltpu.make_async_copy(image_ref.at[t], image_hbm.at[t], sems.at[t]) for t in range(TT)]
+    for t in range(TT):
+        image = dot_nn(carried_ref[t], spatial_ref[t])
+        image_ref[t] = image
+        stores[t].start()
+        product = (probes_ref[t].astype(F32) * image).reshape(WEEKS, PROBES, CELLS)
+        drop_ref[t] = jnp.sum(product, axis=1) * (1.0 / PROBES)
+    last = pltpu.make_async_copy(drop_ref, drop_hbm, sems.at[TT])
+    last.start()
+    for store in stores:
+        store.wait()
+    last.wait()
 
 
 def per_device(probes, spatial, rho, foot_tile, foot_week, footprint, sigma):
@@ -357,14 +365,11 @@
         footprint.reshape(sound * 4, CELLS),
         sigma.reshape(sound // 128, 128),
     )
-    image, drop = pl.pallas_call(
+    carried = pl.pallas_call(
         functools.partial(kernel, ns, nc, sound),
-        out_shape=(
-            jax.ShapeDtypeStruct((TT, WEEKS * PROBES, CELLS), F32),
-            jax.ShapeDtypeStruct((TT, WEEKS, CELLS), F32),
-        ),
+        out_shape=jax.ShapeDtypeStruct((TT, WEEKS * PROBES, CELLS), BF),
         in_specs=[hbm] * 7,
-        out_specs=(vmem, vmem),
+        out_specs=vmem,
         scratch_shapes=[
             pltpu.VMEM((TT, WEEKS * PROBES, CELLS), BF),
             pltpu.VMEM((TT, CELLS, CELLS), BF),
@@ -373,14 +378,13 @@
             pltpu.VMEM((4, sound), jnp.int32),
             pltpu.VMEM((sound * 4, CELLS), BF),
             pltpu.VMEM((sound // 128, 128), F32),
+            pltpu.VMEM((ns * TT, sound), F32),
             pltpu.VMEM((sound // 128, ns * 16, 512), BF),
             pltpu.VMEM((ns * SLOTS, sound), BF),
             pltpu.VMEM((TT, WEEKS * PROBES, CELLS), BF),
             pltpu.VMEM((TT * WEEKS * PROBES, CELLS), F32),
-            pltpu.VMEM((ns, SLOTS, CELLS), BF),
-            pltpu.VMEM((ns, SLOTS, CELLS), BF),
-            pltpu.VMEM((ns, 16, 128), BF),
-            pltpu.VMEM((ns, 16, 128), BF),
+            pltpu.VMEM((ns, SLOTS + 16, CELLS), BF),
+            pltpu.VMEM((ns, SLOTS + 16, CELLS), BF),
             pltpu.VMEM((ns, 16, 128), BF),
             pltpu.VMEM((ns, 16, 128), BF),
             pltpu.VMEM((ns, 16, 128), BF),
@@ -391,13 +395,28 @@
             pltpu.VMEM((nc // 2, PROBES, half), BF),
             pltpu.VMEM((2, PROBES, half), BF),
             dma(7),
-            dma(ns), dma(ns), dma(ns), dma(ns), dma(ns), dma(ns), dma(ns), dma(ns),
+            dma(ns), dma(ns), dma(ns), dma(ns), dma(ns), dma(ns),
             one, one, dma(max(2, nc // 2)), dma(nc // 2), one, one,
         ],
         compiler_params=pltpu.CompilerParams(
             collective_id=0, has_side_effects=True, vmem_limit_bytes=40 * 1024 * 1024
         ),
     )(*(pltpu.with_memory_space_constraint(x, pltpu.HBM) for x in operands))
+    image, drop = pl.pallas_call(
+        finish,
+        out_shape=(
+            jax.ShapeDtypeStruct((TT, WEEKS * PROBES, CELLS), F32),
+            jax.ShapeDtypeStruct((TT, WEEKS, CELLS), F32),
+        ),
+        in_specs=[vmem] * 3,
+        out_specs=(hbm, hbm),
+        scratch_shapes=[
+            pltpu.VMEM((TT, WEEKS * PROBES, CELLS), F32),
+            pltpu.VMEM((TT, WEEKS, CELLS), F32),
+            dma(TT + 1),
+        ],
+        compiler_params=pltpu.CompilerParams(vmem_limit_bytes=4 * 1024 * 1024),
+    )(carried, spatial, probes.reshape(TT, WEEKS * PROBES, CELLS))
     return image.reshape(TT, WEEKS, PROBES, CELLS), drop
 
 

time: 38.4 us -> 37.2 us (0.969)
  local copies, waits for them, and re-layouts: 1.4 us -> 0.01 us
    unnamed x2 -> x4, local copies, waits for them, and re-layouts: 1.4 us -> 0.01 us
    pallas_call x1 -> x2, Pallas kernels: 36.2 us -> 36.4 us  [the longest x1 35.4 us: per_device(): pl.pallas_call(functools.partial(kernel, ns, nc, sound), out_shape=jax.Sh...]
where the time goes in v3:
time: 37.2 us; the launch traced here: 37.1 us
  Pallas kernels  36.4 us (98%)
  between operations  0.67 us (2%)
    pallas_call x1, Pallas kernels, per_device(): pl.pallas_call(functools.partial(kernel, ns, nc, sound), out_shape=jax.Sh...  35.4 us
    pallas_call x1, Pallas kernels, per_device(): pl.pallas_call(finish, out_shape=(jax.ShapeDtypeStruct((TT, WEEKS * PROBE...  1.02 us

profile of v3, /device:TPU:1, one launch (start us, length us, event | category | flops | bytes accessed | tf_op | source)
XLA Modules:
  0.0 37.1 jit_solution(13920452501945798414)
XLA Ops:
  0.6 0.0 copy-start
  0.6 0.0 copy-start.1
  0.7 35.4 %shard_map.86.carried_ref = bf16[8,128,128]{2,1,0:T(8,128)(2,1)S(1)} custom-call(bf16[8,128,128]{2,1,0:T(8,128)(2,1)} %bitcast.6, bf16[8,128,128]{2,1,0:T(8,128)(2,1)} %spatial_ref.1, f32[8]{0:T(128)} %rho_hbm.1, s32[4,1024]{1,0:T(4,128)} %bitcast.9, s32[4,1024]{1,0:T(4,128)} %bitcast.10, bf16[4096,128]{1,0:T(8,128)(2,1)} %bitcast.8, f32[8,128]{1,0:T(8,128)} %bitcast.11), custom_call_target="tpu_custom_call" | custom-call | tf_op jit(solution)/shard_map/pallas_call | solution.py:368
  36.0 0.0 copy-done
  36.0 0.0 copy-done.1
  36.0 1.0 %shard_map.87 = (f32[8,128,128]{2,1,0:T(8,128)}, f32[8,4,128]{2,1,0:T(4,128)}) custom-call(bf16[8,128,128]{2,1,0:T(8,128)(2,1)S(1)} %shard_map.86.carried_ref, bf16[8,128,128]{2,1,0:T(8,128)(2,1)S(1)} %copy-done.1, bf16[8,128,128]{2,1,0:T(8,128)(2,1)S(1)} %bitcast.7), custom_call_target="tpu_custom_call" | custom-call | tf_op jit(solution)/shard_map/pallas_call | solution.py:405
Async XLA Ops:
  0.6 35.4 %copy-start = (bf16[8,4,32,128]{3,2,1,0:T(8,128)(2,1)S(1)}, bf16[8,4,32,128]{3,2,1,0:T(8,128)(2,1)}, u32[]{:S(2)}) copy-start(bf16[8,4,32,128]{3,2,1,0:T(8,128)(2,1)} %param.7) | copy-start | bytes 786436
  0.6 35.4 %copy-start.1 = (bf16[8,128,128]{2,1,0:T(8,128)(2,1)S(1)}, bf16[8,128,128]{2,1,0:T(8,128)(2,1)}, u32[]{:S(2)}) copy-start(bf16[8,128,128]{2,1,0:T(8,128)(2,1)} %spatial_ref.1) | copy-start | bytes 786436

commit v4 on v3

--- a/solution.py
+++ b/solution.py
@@ -61,11 +61,16 @@
     return jnp.concatenate([wide, wide - 1.0], axis=1).reshape(2 * rows, cols).astype(BF)
 
 
-def one_hot(ranks):
-    rows, cols = ranks.shape
-    wide = ranks.reshape(rows // 16, 16, cols)
+def one_hot(*ranks):
+    rows, cols = ranks[0].shape
+    wide = [r.reshape(rows // 16, 16, cols) for r in ranks]
     one, zero = jnp.ones((), BF), jnp.zeros((), BF)
-    rows_of = [jnp.where(wide == jnp.asarray(2 * q, BF), one, zero) for q in range(4)]
+    rows_of = []
+    for q in range(4):
+        same = wide[0] == jnp.asarray(2 * q, BF)
+        for r in wide[1:]:
+            same = same | (r == jnp.asarray(2 * q, BF))
+        rows_of.append(jnp.where(same, one, zero))
     return jnp.concatenate(rows_of, axis=1).reshape(4 * rows, cols)
 
 
@@ -73,7 +78,7 @@
     ns, nc, sound,
     probes_hbm, spatial_hbm, rho_hbm, tile_hbm, week_hbm, foot_hbm, sigma_hbm,
     carried_ref,
-    probes_ref, spatial_ref, rho_ref, tile_ref, week_ref, foot_ref, sigma_ref, order_ref, ranks_ref, hot_ref, field_ref, adjoint_ref,
+    probes_ref, spatial_ref, rho_ref, tile_ref, week_ref, foot_ref, sigma_ref, order_ref, early_ref, ranks_ref, hot_ref, field_ref,
     send_f, recv_f, send_v, recv_v, send_p, recv_p,
     send_c, recv_c, send_y, recv_y, recv_w,
     load_sem, ss_f, rs_f, ss_v, rs_v, ss_p, rs_p, ss_c, rs_c, ss_y, rs_y, ss_w, rs_w,
@@ -155,6 +160,12 @@
             if (dx, dz) != (0, 0):
                 from_snd(refs, partner(dx, dz)).wait_recv()
 
+    def sent(refs):
+        for dx in far:
+            for dz in far_z:
+                if (dx, dz) != (0, 0):
+                    to_snd(refs, partner(dx, dz)).wait_send()
+
     def group_rows(dx, size):
         return pl.ds(pl.multiple_of(group_x(dx) * 4 * size, 4 * size), 4 * size)
 
@@ -166,33 +177,36 @@
     tiles = tile_ref[...]
     weeks = week_ref[...]
     shift = nc.bit_length() - 1
-    row_j = iota((nj, 256), 0)
-    upper = jnp.where(iota((256, 256), 0) < iota((256, 256), 1), 1.0, 0.0).astype(BF)
-    counts = jnp.concatenate([upper, jnp.ones((256, 256), BF)], axis=1)
+    width = min(256, sound // 2)
+    row_j = iota((nj, width), 0)
+    upper = jnp.where(iota((width, width), 0) < iota((width, width), 1), 1.0, 0.0).astype(BF)
+    counts = jnp.concatenate([upper, jnp.ones((width, width), BF)], axis=1)
     spread_e = jnp.where(iota((128, 512), 0) == iota((128, 512), 1) >> 2, 1.0, 0.0).astype(BF)
     pick_k = (iota((WEEKS, 512), 1) & 3) == iota((WEEKS, 512), 0)
     row_e = iota((nj, 512), 0).astype(F32)
 
     matched = ((tiles >> 3) & (nc - 1)) == mine
     local = jnp.where(matched, ((tiles >> (3 + shift)) << 3) | (tiles & 7), -1)
-    carry = jnp.zeros((nj, 256), F32)
-    bits = jnp.zeros((nj, 256), F32)
-    for b in range(sound // 256):
-        lanes = slice(256 * b, 256 * b + 256)
-        named = jnp.zeros((nj, 256), F32)
-        week_of = jnp.zeros((nj, 256), jnp.int32)
+    carry = jnp.zeros((nj, width), F32)
+    bits = jnp.zeros((nj, width), F32)
+    for b in range(sound // width):
+        if 2 * width * b == sound:
+            early_ref[...] = carry[:, :128]
+        lanes = slice(width * b, width * b + width)
+        named = jnp.zeros((nj, width), F32)
+        week_of = jnp.zeros((nj, width), jnp.int32)
         for k in range(4):
             same = local[k : k + 1, lanes] == row_j
             named = jnp.where(same, 1.0, named)
             week_of = jnp.where(same, weeks[k : k + 1, lanes], week_of)
         counted = dot_nn(named.astype(BF), counts)
-        place = counted[:, :256] + carry
+        place = counted[:, :width] + carry
         order = jnp.where(named > 0.0, place, -1.0)
-        carry = carry + counted[:, 256:]
+        carry = carry + counted[:, width:]
         bits = bits + (week_of << (place.astype(jnp.int32) * 2)).astype(F32)
         order_ref[:, lanes] = order
-        for part in range(2):
-            a = 2 * b + part
+        for part in range(width // 128):
+            a = width // 128 * b + part
             here = slice(128 * a, 128 * a + 128)
             spread_rank = dot_nn(order[:, 128 * part : 128 * part + 128].astype(BF), spread_e)
             spread_tile = dot_nn(local[:, here].astype(F32).astype(BF), spread_e)
@@ -209,11 +223,18 @@
 
     loads[2].wait()
 
+    both = jnp.concatenate([foot_ref[: 2 * sound, :], foot_ref[2 * sound :, :]], axis=1)
+    pairs = sound // 256
+
     def pick_feet(dx):
-        total = jnp.zeros((256, CELLS), F32)
-        for a in range(sound // 128):
-            total = total + dot_nn(one_hot(ranks_ref[a, group_rows(dx, 16), :]), foot_ref[512 * a : 512 * a + 512, :])
-        send_f[group_of(dx), :SLOTS] = total.astype(BF).reshape(4, SLOTS, CELLS)
+        for part in range(2):
+            first = group_x(dx) * 4 + 2 * part
+            rows = pl.ds(pl.multiple_of(first * 16, 32), 32)
+            picks = [one_hot(ranks_ref[a, rows, :], ranks_ref[a + pairs, rows, :]) for a in range(pairs)]
+            found = dot_nn(jnp.concatenate(picks, axis=1), both).reshape(2, 8, TT, 2 * CELLS)
+            early = early_ref[pl.ds(pl.multiple_of(first * TT, 16), 16), :].reshape(2, TT, CELLS)
+            kept = [jnp.where(early > float(r), found[:, r, :, :CELLS], found[:, r, :, CELLS:]) for r in range(8)]
+            send_f[pl.ds(first, 2), :SLOTS] = jnp.stack(kept, axis=1).reshape(2, SLOTS, CELLS).astype(BF)
 
     for dx in far[:-1]:
         pick_feet(dx)
@@ -245,6 +266,7 @@
     codes = {}
     for dx in near:
         wait_group(of_f, dx)
+    for dx in near:
         names = recv_f[group_of(dx), SLOTS:].astype(F32)
         low = low_half(16)
         code = jnp.concatenate([jnp.where(low, names[0], names[1]), jnp.where(low, names[2], names[3])], axis=1)
@@ -258,11 +280,15 @@
                 here = jnp.where(lane_tile == t, full[t, w], here)
             value = jnp.where(codes[dx] == float(w), here, value)
         send_v[group_of(dx)] = packed(value)
+    for dx in far:
         send_group(of_v, dx)
+
+    sent(of_f)
 
     seen = jnp.zeros((PROBES, sound), F32)
     for dx in near:
         wait_group(of_v, dx)
+    for dx in near:
         seen = seen + dot_nn(unpacked(recv_v[group_of(dx)]).astype(BF), hot_ref[group_rows(dx, SLOTS), :])
     send_c[0] = seen[:, :half]
     send_c[1] = seen[:, half:]
@@ -285,8 +311,11 @@
     steps_y = {1: [], 2: [1], 4: [2, 1, 3]}[ny]
     for dy in steps_y:
         over_y(dy, row_y).start()
+    sent(of_v)
+    swap.wait_send()
     for dy in reversed(steps_y):
         over_y(dy, (row_y + dy) % ny).wait_recv()
+    for dy in reversed(steps_y):
         total = total + recv_y[(row_y + dy) % ny].astype(F32)
     own = half // 128
     sigma = jnp.concatenate([sigma_ref[pl.ds(core * own + i, 1), :] for i in range(own)], axis=1)
@@ -299,38 +328,34 @@
     share.wait_recv()
 
     weighted = jnp.concatenate([recv_w[0], recv_w[1]], axis=1)
+    backs = dot_nt(weighted, hot_ref[...])
+    for x in range(groups):
+        send_p[4 * x : 4 * x + 4] = packed(backs[:, 256 * x : 256 * x + 256])
     for dx in far:
-        send_p[group_of(dx)] = packed(dot_nt(weighted, hot_ref[group_rows(dx, SLOTS), :]))
         send_group(of_p, dx)
 
-    for step, dx in enumerate(near):
+    for dy in steps_y:
+        over_y(dy, row_y).wait_send()
+
+    at_tile = [lane_tile.astype(F32).astype(BF) == jnp.asarray(t, BF) for t in range(TT)]
+    by_week = []
+    for dx in near:
         wait_group(of_p, dx)
-        value = unpacked(recv_p[group_of(dx)])
-        by_week = [jnp.where(codes[dx] == float(w), value, 0.0) for w in range(WEEKS)]
-        spread = [jnp.where(lane_tile == t, by_week[w], 0.0).astype(BF) for t in range(TT) for w in range(WEEKS)]
-        adjoint = dot_nn(jnp.concatenate(spread, axis=0), recv_f[group_of(dx), :SLOTS].reshape(256, CELLS))
-        if step > 0:
-            adjoint = adjoint + adjoint_ref[...]
-        if step < groups - 1:
-            adjoint_ref[...] = adjoint
+        value, code = unpacked(recv_p[group_of(dx)]).astype(BF), codes[dx].astype(BF)
+        by_week.append([jnp.where(code == jnp.asarray(w, BF), value, jnp.zeros((), BF)) for w in range(WEEKS)])
+    feet = jnp.concatenate([recv_f[group_of(dx), :SLOTS].reshape(256, CELLS) for dx in near], axis=0)
     for t in range(TT):
-        rows = WEEKS * PROBES * t
-        running = adjoint[rows + PROBES * (WEEKS - 1) : rows + PROBES * WEEKS]
+        spread = [jnp.concatenate([jnp.where(at_tile[t], part, jnp.zeros((), BF)) for part in weeks_of], axis=0) for weeks_of in by_week]
+        adjoint = dot_nn(jnp.concatenate(spread, axis=1), feet)
+        running = adjoint[PROBES * (WEEKS - 1) :]
         carried = [running]
         for w in range(WEEKS - 2, -1, -1):
-            running = adjoint[rows + PROBES * w : rows + PROBES * w + PROBES] + rho_ref[t] * running
+            running = adjoint[PROBES * w : PROBES * w + PROBES] + rho_ref[t] * running
             carried.append(running)
         carried_ref[t] = jnp.concatenate(carried[::-1], axis=0).astype(BF)
 
-    for refs in (of_f, of_v, of_p):
-        for dx in far:
-            for dz in far_z:
-                if (dx, dz) != (0, 0):
-                    to_snd(refs, partner(dx, dz)).wait_send()
-    swap.wait_send()
+    sent(of_p)
     share.wait_send()
-    for dy in steps_y:
-        over_y(dy, row_y).wait_send()
 
 
 def finish(carried_ref, spatial_ref, probes_ref, image_hbm, drop_hbm, image_ref, drop_ref, sems):
@@ -379,10 +404,10 @@
             pltpu.VMEM((sound * 4, CELLS), BF),
             pltpu.VMEM((sound // 128, 128), F32),
             pltpu.VMEM((ns * TT, sound), F32),
+            pltpu.VMEM((ns * TT, 128), F32),
             pltpu.VMEM((sound // 128, ns * 16, 512), BF),
             pltpu.VMEM((ns * SLOTS, sound), BF),
             pltpu.VMEM((TT, WEEKS * PROBES, CELLS), BF),
-            pltpu.VMEM((TT * WEEKS * PROBES, CELLS), F32),
             pltpu.VMEM((ns, SLOTS + 16, CELLS), BF),
             pltpu.VMEM((ns, SLOTS + 16, CELLS), BF),
             pltpu.VMEM((ns, 16, 128), BF),

time: 37.2 us -> 34.8 us (0.935)
  Pallas kernels: 36.4 us -> 34 us
    pallas_call x1, Pallas kernels: 35.4 us -> 33 us  [per_device(): pl.pallas_call(functools.partial(kernel, ns, nc, sound), out_shape=jax.Sh...]
where the time goes in v4:
time: 34.8 us; the launch traced here: 34.7 us
  Pallas kernels  34 us (98%)
  between operations  0.67 us (2%)
    pallas_call x1, Pallas kernels, per_device(): pl.pallas_call(functools.partial(kernel, ns, nc, sound), out_shape=jax.Sh...  33 us
    pallas_call x1, Pallas kernels, per_device(): pl.pallas_call(finish, out_shape=(jax.ShapeDtypeStruct((TT, WEEKS * PROBE...  1.02 us

profile of v4, /device:TPU:1, one launch (start us, length us, event | category | flops | bytes accessed | tf_op | source)
XLA Modules:
  0.0 34.7 jit_solution(7657081395983686233)
XLA Ops:
  0.6 0.0 copy-start
  0.6 0.0 copy-start.1
  0.7 33.0 %shard_map.86.carried_ref = bf16[8,128,128]{2,1,0:T(8,128)(2,1)S(1)} custom-call(bf16[8,128,128]{2,1,0:T(8,128)(2,1)} %bitcast.6, bf16[8,128,128]{2,1,0:T(8,128)(2,1)} %spatial_ref.1, f32[8]{0:T(128)} %rho_hbm.1, s32[4,1024]{1,0:T(4,128)} %bitcast.9, s32[4,1024]{1,0:T(4,128)} %bitcast.10, bf16[4096,128]{1,0:T(8,128)(2,1)} %bitcast.8, f32[8,128]{1,0:T(8,128)} %bitcast.11), custom_call_target="tpu_custom_call" | custom-call | tf_op jit(solution)/shard_map/pallas_call | solution.py:393
  33.7 0.0 copy-done
  33.7 0.0 copy-done.1
  33.7 1.0 %shard_map.87 = (f32[8,128,128]{2,1,0:T(8,128)}, f32[8,4,128]{2,1,0:T(4,128)}) custom-call(bf16[8,128,128]{2,1,0:T(8,128)(2,1)S(1)} %shard_map.86.carried_ref, bf16[8,128,128]{2,1,0:T(8,128)(2,1)S(1)} %copy-done.1, bf16[8,128,128]{2,1,0:T(8,128)(2,1)S(1)} %bitcast.7), custom_call_target="tpu_custom_call" | custom-call | tf_op jit(solution)/shard_map/pallas_call | solution.py:430
Async XLA Ops:
  0.6 33.0 %copy-start = (bf16[8,4,32,128]{3,2,1,0:T(8,128)(2,1)S(1)}, bf16[8,4,32,128]{3,2,1,0:T(8,128)(2,1)}, u32[]{:S(2)}) copy-start(bf16[8,4,32,128]{3,2,1,0:T(8,128)(2,1)} %param.7) | copy-start | bytes 786436
  0.6 33.0 %copy-start.1 = (bf16[8,128,128]{2,1,0:T(8,128)(2,1)S(1)}, bf16[8,128,128]{2,1,0:T(8,128)(2,1)}, u32[]{:S(2)}) copy-start(bf16[8,128,128]{2,1,0:T(8,128)(2,1)} %spatial_ref.1) | copy-start | bytes 786436

commit v5 on v4

--- a/solution.py
+++ b/solution.py
@@ -16,6 +16,7 @@
 WEEKS = 4
 PROBES = 32
 CELLS = 128
+SIDE = 2
 
 
 def dot_nn(a, b):
@@ -78,7 +79,7 @@
     ns, nc, sound,
     probes_hbm, spatial_hbm, rho_hbm, tile_hbm, week_hbm, foot_hbm, sigma_hbm,
     carried_ref,
-    probes_ref, spatial_ref, rho_ref, tile_ref, week_ref, foot_ref, sigma_ref, order_ref, early_ref, ranks_ref, hot_ref, field_ref,
+    probes_ref, spatial_ref, rho_ref, tile_ref, week_ref, foot_ref, sigma_ref, order_ref, early_ref, ranks_ref, hot_ref, field_ref, wide_ref,
     send_f, recv_f, send_v, recv_v, send_p, recv_p,
     send_c, recv_c, send_y, recv_y, recv_w,
     load_sem, ss_f, rs_f, ss_v, rs_v, ss_p, rs_p, ss_c, rs_c, ss_y, rs_y, ss_w, rs_w,
@@ -131,18 +132,12 @@
         greet(me, (row_y + dy) % ny * 2 + core)
     greet(me, row_y * 2 + 1 - core)
 
-    def over_snd(refs, there, here, other):
+    def to_snd(refs, dest):
         src, dst, ss, rs = refs
         return pltpu.make_async_remote_copy(
-            src_ref=src.at[there], dst_ref=dst.at[here], send_sem=ss.at[there], recv_sem=rs.at[here],
-            device_id={"snd": other, "cell": mine}, device_id_type=MESH,
+            src_ref=src.at[dest], dst_ref=dst.at[me], send_sem=ss, recv_sem=rs,
+            device_id={"snd": dest, "cell": mine}, device_id_type=MESH,
         )
-
-    def to_snd(refs, dest):
-        return over_snd(refs, dest, me, dest)
-
-    def from_snd(refs, source):
-        return over_snd(refs, source, source, source)
 
     of_f = (send_f, recv_f, ss_f, rs_f)
     of_v = (send_v, recv_v, ss_v, rs_v)
@@ -155,16 +150,14 @@
         if dx == 0:
             refs[1][me] = refs[0][me]
 
-    def wait_group(refs, dx):
-        for dz in range(4):
-            if (dx, dz) != (0, 0):
-                from_snd(refs, partner(dx, dz)).wait_recv()
+    def of_others(buffer, sem):
+        pltpu.make_async_copy(buffer.at[pl.ds(0, ns - 1)], buffer.at[pl.ds(0, ns - 1)], sem).wait()
+
+    def arrived(refs):
+        of_others(refs[1], refs[3])
 
     def sent(refs):
-        for dx in far:
-            for dz in far_z:
-                if (dx, dz) != (0, 0):
-                    to_snd(refs, partner(dx, dz)).wait_send()
+        of_others(refs[0], refs[2])
 
     def group_rows(dx, size):
         return pl.ds(pl.multiple_of(group_x(dx) * 4 * size, 4 * size), 4 * size)
@@ -255,29 +248,34 @@
         load.wait()
     for t in range(TT):
         spread = dot_nt(probes_ref[t], spatial_ref[t])
+        lanes = slice(CELLS * (t % SIDE), CELLS * (t % SIDE) + CELLS)
         running = spread[:PROBES]
-        field_ref[t, :PROBES] = running.astype(BF)
+        field_ref[t // SIDE, :PROBES, lanes] = running.astype(BF)
         for w in range(1, WEEKS):
             running = spread[PROBES * w : PROBES * w + PROBES] + rho_ref[t] * running
-            field_ref[t, PROBES * w : PROBES * w + PROBES] = running.astype(BF)
-
-    lane_tile = iota((PROBES, 256), 1) & 7
-    fields = field_ref[...].reshape(TT * WEEKS * PROBES, CELLS)
+            field_ref[t // SIDE, PROBES * w : PROBES * w + PROBES, lanes] = running.astype(BF)
+
+    lane_side = (iota((PROBES, 256), 1) & 7) // SIDE
+    row_tile = (iota((256, CELLS), 0) & (SIDE - 1)).astype(F32).astype(BF)
+    fields = field_ref[...].reshape(TT // SIDE * WEEKS * PROBES, SIDE * CELLS)
     codes = {}
-    for dx in near:
-        wait_group(of_f, dx)
+    arrived(of_f)
     for dx in near:
         names = recv_f[group_of(dx), SLOTS:].astype(F32)
         low = low_half(16)
         code = jnp.concatenate([jnp.where(low, names[0], names[1]), jnp.where(low, names[2], names[3])], axis=1)
         codes[dx] = jnp.concatenate([code, code], axis=0)
-        full = dot_nt(fields, recv_f[group_of(dx), :SLOTS].reshape(256, CELLS))
-        full = full.reshape(TT, WEEKS, PROBES, 256)
+        feet = recv_f[group_of(dx), :SLOTS].reshape(256, CELLS)
+        sides = [jnp.where(row_tile == jnp.asarray(h, BF), feet, jnp.zeros((), BF)) for h in range(SIDE)]
+        wide = jnp.concatenate(sides, axis=1)
+        wide_ref[group_rows(dx, SLOTS), :] = wide
+        full = dot_nt(fields, wide)
+        full = full.reshape(TT // SIDE, WEEKS, PROBES, 256)
         value = jnp.zeros((PROBES, 256), F32)
         for w in range(WEEKS):
             here = full[0, w]
-            for t in range(1, TT):
-                here = jnp.where(lane_tile == t, full[t, w], here)
+            for g in range(1, TT // SIDE):
+                here = jnp.where(lane_side == g, full[g, w], here)
             value = jnp.where(codes[dx] == float(w), here, value)
         send_v[group_of(dx)] = packed(value)
     for dx in far:
@@ -286,8 +284,7 @@
     sent(of_f)
 
     seen = jnp.zeros((PROBES, sound), F32)
-    for dx in near:
-        wait_group(of_v, dx)
+    arrived(of_v)
     for dx in near:
         seen = seen + dot_nn(unpacked(recv_v[group_of(dx)]).astype(BF), hot_ref[group_rows(dx, SLOTS), :])
     send_c[0] = seen[:, :half]
@@ -337,22 +334,25 @@
     for dy in steps_y:
         over_y(dy, row_y).wait_send()
 
-    at_tile = [lane_tile.astype(F32).astype(BF) == jnp.asarray(t, BF) for t in range(TT)]
-    by_week = []
+    at_side = [lane_side.astype(F32).astype(BF) == jnp.asarray(g, BF) for g in range(TT // SIDE)]
+    arrived(of_p)
+    spread = []
     for dx in near:
-        wait_group(of_p, dx)
         value, code = unpacked(recv_p[group_of(dx)]).astype(BF), codes[dx].astype(BF)
-        by_week.append([jnp.where(code == jnp.asarray(w, BF), value, jnp.zeros((), BF)) for w in range(WEEKS)])
-    feet = jnp.concatenate([recv_f[group_of(dx), :SLOTS].reshape(256, CELLS) for dx in near], axis=0)
-    for t in range(TT):
-        spread = [jnp.concatenate([jnp.where(at_tile[t], part, jnp.zeros((), BF)) for part in weeks_of], axis=0) for weeks_of in by_week]
-        adjoint = dot_nn(jnp.concatenate(spread, axis=1), feet)
-        running = adjoint[PROBES * (WEEKS - 1) :]
-        carried = [running]
-        for w in range(WEEKS - 2, -1, -1):
-            running = adjoint[PROBES * w : PROBES * w + PROBES] + rho_ref[t] * running
-            carried.append(running)
-        carried_ref[t] = jnp.concatenate(carried[::-1], axis=0).astype(BF)
+        by_week = [jnp.where(code == jnp.asarray(w, BF), value, jnp.zeros((), BF)) for w in range(WEEKS)]
+        spread.append([[jnp.where(at, part, jnp.zeros((), BF)) for part in by_week] for at in at_side])
+    feet = jnp.concatenate([wide_ref[group_rows(dx, SLOTS), :] for dx in near], axis=0)
+    for g in range(TT // SIDE):
+        kept = jnp.concatenate([jnp.concatenate(parts[g], axis=0) for parts in spread], axis=1)
+        adjoint = dot_nn(kept, feet)
+        for h in range(SIDE):
+            here = adjoint[:, CELLS * h : CELLS * h + CELLS]
+            running = here[PROBES * (WEEKS - 1) :]
+            carried = [running]
+            for w in range(WEEKS - 2, -1, -1):
+                running = here[PROBES * w : PROBES * w + PROBES] + rho_ref[SIDE * g + h] * running
+                carried.append(running)
+            carried_ref[SIDE * g + h] = jnp.concatenate(carried[::-1], axis=0).astype(BF)
 
     sent(of_p)
     share.wait_send()
@@ -407,7 +407,8 @@
             pltpu.VMEM((ns * TT, 128), F32),
             pltpu.VMEM((sound // 128, ns * 16, 512), BF),
             pltpu.VMEM((ns * SLOTS, sound), BF),
-            pltpu.VMEM((TT, WEEKS * PROBES, CELLS), BF),
+            pltpu.VMEM((TT // SIDE, WEEKS * PROBES, SIDE * CELLS), BF),
+            pltpu.VMEM((ns * SLOTS, SIDE * CELLS), BF),
             pltpu.VMEM((ns, SLOTS + 16, CELLS), BF),
             pltpu.VMEM((ns, SLOTS + 16, CELLS), BF),
             pltpu.VMEM((ns, 16, 128), BF),
@@ -420,7 +421,7 @@
             pltpu.VMEM((nc // 2, PROBES, half), BF),
             pltpu.VMEM((2, PROBES, half), BF),
             dma(7),
-            dma(ns), dma(ns), dma(ns), dma(ns), dma(ns), dma(ns),
+            one, one, one, one, one, one,
             one, one, dma(max(2, nc // 2)), dma(nc // 2), one, one,
         ],
         compiler_params=pltpu.CompilerParams(

time: 34.8 us -> 33.6 us (0.966)
  Pallas kernels: 34 us -> 32.8 us
    pallas_call x1, Pallas kernels: 33 us -> 31.7 us  [per_device(): pl.pallas_call(functools.partial(kernel, ns, nc, sound), out_shape=jax.Sh...]
where the time goes in v5:
time: 33.6 us; the launch traced here: 33.4 us
  Pallas kernels  32.8 us (98%)
  between operations  0.67 us (2%)
    pallas_call x1, Pallas kernels, per_device(): pl.pallas_call(functools.partial(kernel, ns, nc, sound), out_shape=jax.Sh...  31.7 us
    pallas_call x1, Pallas kernels, per_device(): pl.pallas_call(finish, out_shape=(jax.ShapeDtypeStruct((TT, WEEKS * PROBE...  1.02 us

profile of v5, /device:TPU:1, one launch (start us, length us, event | category | flops | bytes accessed | tf_op | source)
XLA Modules:
  0.0 33.4 jit_solution(8055276569052675260)
XLA Ops:
  0.6 0.0 copy-start
  0.6 0.0 copy-start.1
  0.7 31.7 %shard_map.86.carried_ref = bf16[8,128,128]{2,1,0:T(8,128)(2,1)S(1)} custom-call(bf16[8,128,128]{2,1,0:T(8,128)(2,1)} %bitcast.6, bf16[8,128,128]{2,1,0:T(8,128)(2,1)} %spatial_ref.1, f32[8]{0:T(128)} %rho_hbm.1, s32[4,1024]{1,0:T(4,128)} %bitcast.9, s32[4,1024]{1,0:T(4,128)} %bitcast.10, bf16[4096,128]{1,0:T(8,128)(2,1)} %bitcast.8, f32[8,128]{1,0:T(8,128)} %bitcast.11), custom_call_target="tpu_custom_call" | custom-call | tf_op jit(solution)/shard_map/pallas_call | solution.py:393
  32.4 0.0 copy-done
  32.4 0.0 copy-done.1
  32.4 1.0 %shard_map.87 = (f32[8,128,128]{2,1,0:T(8,128)}, f32[8,4,128]{2,1,0:T(4,128)}) custom-call(bf16[8,128,128]{2,1,0:T(8,128)(2,1)S(1)} %shard_map.86.carried_ref, bf16[8,128,128]{2,1,0:T(8,128)(2,1)S(1)} %copy-done.1, bf16[8,128,128]{2,1,0:T(8,128)(2,1)S(1)} %bitcast.7), custom_call_target="tpu_custom_call" | custom-call | tf_op jit(solution)/shard_map/pallas_call | solution.py:431
Async XLA Ops:
  0.6 31.8 %copy-start = (bf16[8,4,32,128]{3,2,1,0:T(8,128)(2,1)S(1)}, bf16[8,4,32,128]{3,2,1,0:T(8,128)(2,1)}, u32[]{:S(2)}) copy-start(bf16[8,4,32,128]{3,2,1,0:T(8,128)(2,1)} %param.7) | copy-start | bytes 786436
  0.6 31.8 %copy-start.1 = (bf16[8,128,128]{2,1,0:T(8,128)(2,1)S(1)}, bf16[8,128,128]{2,1,0:T(8,128)(2,1)}, u32[]{:S(2)}) copy-start(bf16[8,128,128]{2,1,0:T(8,128)(2,1)} %spatial_ref.1) | copy-start | bytes 786436

commit v6 on v5

--- a/solution.py
+++ b/solution.py
@@ -80,9 +80,9 @@
     probes_hbm, spatial_hbm, rho_hbm, tile_hbm, week_hbm, foot_hbm, sigma_hbm,
     carried_ref,
     probes_ref, spatial_ref, rho_ref, tile_ref, week_ref, foot_ref, sigma_ref, order_ref, early_ref, ranks_ref, hot_ref, field_ref, wide_ref,
-    send_f, recv_f, send_v, recv_v, send_p, recv_p,
+    send_f, recv_f, send_k, recv_k, send_v, recv_v, send_p, recv_p,
     send_c, recv_c, send_y, recv_y, recv_w,
-    load_sem, ss_f, rs_f, ss_v, rs_v, ss_p, rs_p, ss_c, rs_c, ss_y, rs_y, ss_w, rs_w,
+    load_sem, ss_f, rs_f, ss_k, rs_k, ss_v, rs_v, ss_p, rs_p, ss_c, rs_c, ss_y, rs_y, ss_w, rs_w,
 ):
     me = lax.axis_index("snd")
     mine = lax.axis_index("cell")
@@ -140,6 +140,7 @@
         )
 
     of_f = (send_f, recv_f, ss_f, rs_f)
+    of_k = (send_k, recv_k, ss_k, rs_k)
     of_v = (send_v, recv_v, ss_v, rs_v)
     of_p = (send_p, recv_p, ss_p, rs_p)
 
@@ -212,7 +213,7 @@
         word = jnp.broadcast_to(bits[TT * d : TT * d + TT], (TT, 128))
         week = (word >> (((lane & 63) >> 3) * 2)) & 3
         row = jnp.sum(jnp.where((lane & 7) == iota((TT, 128), 0), week.astype(F32), 0.0), axis=0, keepdims=True)
-        send_f[d, SLOTS:] = jnp.broadcast_to(row, (16, 128)).astype(BF)
+        send_k[d] = row
 
     loads[2].wait()
 
@@ -227,18 +228,21 @@
             found = dot_nn(jnp.concatenate(picks, axis=1), both).reshape(2, 8, TT, 2 * CELLS)
             early = early_ref[pl.ds(pl.multiple_of(first * TT, 16), 16), :].reshape(2, TT, CELLS)
             kept = [jnp.where(early > float(r), found[:, r, :, :CELLS], found[:, r, :, CELLS:]) for r in range(8)]
-            send_f[pl.ds(first, 2), :SLOTS] = jnp.stack(kept, axis=1).reshape(2, SLOTS, CELLS).astype(BF)
-
-    for dx in far[:-1]:
+            send_f[pl.ds(first, 2)] = jnp.stack(kept, axis=1).reshape(2, SLOTS, CELLS).astype(BF)
+
+    for dx in far[: groups // 2]:
         pick_feet(dx)
     if groups == 1:
         pick_feet(0)
     pl.semaphore_wait(barrier, ns - 1 + ny - 1 + 1)
-    for dx in far[:-1]:
+    for dx in far:
+        send_group(of_k, dx)
+    for dx in far[: groups // 2]:
         send_group(of_f, dx)
-    if groups > 1:
-        pick_feet(0)
-    send_group(of_f, 0)
+    for dx in far[groups // 2 :]:
+        if groups > 1:
+            pick_feet(dx)
+        send_group(of_f, dx)
 
     for b in range(sound // 256):
         lanes = slice(256 * b, 256 * b + 256)
@@ -260,12 +264,13 @@
     fields = field_ref[...].reshape(TT // SIDE * WEEKS * PROBES, SIDE * CELLS)
     codes = {}
     arrived(of_f)
+    arrived(of_k)
     for dx in near:
-        names = recv_f[group_of(dx), SLOTS:].astype(F32)
-        low = low_half(16)
+        names = recv_k[group_of(dx)]
+        low = low_half(1)
         code = jnp.concatenate([jnp.where(low, names[0], names[1]), jnp.where(low, names[2], names[3])], axis=1)
-        codes[dx] = jnp.concatenate([code, code], axis=0)
-        feet = recv_f[group_of(dx), :SLOTS].reshape(256, CELLS)
+        codes[dx] = jnp.broadcast_to(code, (PROBES, 256))
+        feet = recv_f[group_of(dx)].reshape(256, CELLS)
         sides = [jnp.where(row_tile == jnp.asarray(h, BF), feet, jnp.zeros((), BF)) for h in range(SIDE)]
         wide = jnp.concatenate(sides, axis=1)
         wide_ref[group_rows(dx, SLOTS), :] = wide
@@ -282,6 +287,7 @@
         send_group(of_v, dx)
 
     sent(of_f)
+    sent(of_k)
 
     seen = jnp.zeros((PROBES, sound), F32)
     arrived(of_v)
@@ -409,8 +415,10 @@
             pltpu.VMEM((ns * SLOTS, sound), BF),
             pltpu.VMEM((TT // SIDE, WEEKS * PROBES, SIDE * CELLS), BF),
             pltpu.VMEM((ns * SLOTS, SIDE * CELLS), BF),
-            pltpu.VMEM((ns, SLOTS + 16, CELLS), BF),
-            pltpu.VMEM((ns, SLOTS + 16, CELLS), BF),
+            pltpu.VMEM((ns, SLOTS, CELLS), BF),
+            pltpu.VMEM((ns, SLOTS, CELLS), BF),
+            pltpu.VMEM((ns, 1, 128), F32),
+            pltpu.VMEM((ns, 1, 128), F32),
             pltpu.VMEM((ns, 16, 128), BF),
             pltpu.VMEM((ns, 16, 128), BF),
             pltpu.VMEM((ns, 16, 128), BF),
@@ -421,7 +429,7 @@
             pltpu.VMEM((nc // 2, PROBES, half), BF),
             pltpu.VMEM((2, PROBES, half), BF),
             dma(7),
-            one, one, one, one, one, one,
+            one, one, one, one, one, one, one, one,
             one, one, dma(max(2, nc // 2)), dma(nc // 2), one, one,
         ],
         compiler_params=pltpu.CompilerParams(

time: 33.6 us -> 33 us (0.982)
  Pallas kernels: 32.8 us -> 32.2 us
    pallas_call x1, Pallas kernels: 31.7 us -> 31.2 us  [per_device(): pl.pallas_call(functools.partial(kernel, ns, nc, sound), out_shape=jax.Sh...]
where the time goes in v6:
time: 33 us; the launch traced here: 32.9 us
  Pallas kernels  32.2 us (98%)
  between operations  0.67 us (2%)
    pallas_call x1, Pallas kernels, per_device(): pl.pallas_call(functools.partial(kernel, ns, nc, sound), out_shape=jax.Sh...  31.2 us
    pallas_call x1, Pallas kernels, per_device(): pl.pallas_call(finish, out_shape=(jax.ShapeDtypeStruct((TT, WEEKS * PROBE...  1.02 us

profile of v6, /device:TPU:1, one launch (start us, length us, event | category | flops | bytes accessed | tf_op | source)
XLA Modules:
  0.0 32.9 jit_solution(18134973061024028147)
XLA Ops:
  0.6 0.0 copy-start
  0.6 0.0 copy-start.1
  0.7 31.2 %shard_map.86.carried_ref = bf16[8,128,128]{2,1,0:T(8,128)(2,1)S(1)} custom-call(bf16[8,128,128]{2,1,0:T(8,128)(2,1)} %bitcast.6, bf16[8,128,128]{2,1,0:T(8,128)(2,1)} %spatial_ref.1, f32[8]{0:T(128)} %rho_hbm.1, s32[4,1024]{1,0:T(4,128)} %bitcast.9, s32[4,1024]{1,0:T(4,128)} %bitcast.10, bf16[4096,128]{1,0:T(8,128)(2,1)} %bitcast.8, f32[8,128]{1,0:T(8,128)} %bitcast.11), custom_call_target="tpu_custom_call" | custom-call | tf_op jit(solution)/shard_map/pallas_call | solution.py:399
  31.8 0.0 copy-done
  31.8 0.0 copy-done.1
  31.9 1.0 %shard_map.87 = (f32[8,128,128]{2,1,0:T(8,128)}, f32[8,4,128]{2,1,0:T(4,128)}) custom-call(bf16[8,128,128]{2,1,0:T(8,128)(2,1)S(1)} %shard_map.86.carried_ref, bf16[8,128,128]{2,1,0:T(8,128)(2,1)S(1)} %copy-done.1, bf16[8,128,128]{2,1,0:T(8,128)(2,1)S(1)} %bitcast.7), custom_call_target="tpu_custom_call" | custom-call | tf_op jit(solution)/shard_map/pallas_call | solution.py:439
Async XLA Ops:
  0.6 31.2 %copy-start = (bf16[8,4,32,128]{3,2,1,0:T(8,128)(2,1)S(1)}, bf16[8,4,32,128]{3,2,1,0:T(8,128)(2,1)}, u32[]{:S(2)}) copy-start(bf16[8,4,32,128]{3,2,1,0:T(8,128)(2,1)} %param.7) | copy-start | bytes 786436
  0.6 31.2 %copy-start.1 = (bf16[8,128,128]{2,1,0:T(8,128)(2,1)S(1)}, bf16[8,128,128]{2,1,0:T(8,128)(2,1)}, u32[]{:S(2)}) copy-start(bf16[8,128,128]{2,1,0:T(8,128)(2,1)} %spatial_ref.1) | copy-start | bytes 786436

commit v7 on v6

--- a/solution.py
+++ b/solution.py
@@ -86,12 +86,12 @@
 ):
     me = lax.axis_index("snd")
     mine = lax.axis_index("cell")
-    core, row_y = mine % 2, mine // 2
+    core, row_y = lax.rem(mine, 2), lax.div(mine, 2)
     nj = ns * TT
     groups = ns // 4
     ny = nc // 2
     half = sound // 2
-    mx, mz = me // 4, me % 4
+    mx, mz = lax.div(me, 4), lax.rem(me, 4)
     near = {1: [0], 2: [0, 1], 4: [0, 1, 3, 2]}[groups]
     far = near[::-1]
     far_z = [2, 1, 3, 0]
@@ -119,17 +119,17 @@
         pl.semaphore_signal(barrier, inc=1, device_id={"snd": snd, "cell": cell}, device_id_type=MESH)
 
     def group_x(dx):
-        return (mx + dx) % groups
+        return lax.rem(mx + dx, groups)
 
     def partner(dx, dz):
-        return group_x(dx) * 4 + (mz + dz) % 4
+        return group_x(dx) * 4 + lax.rem(mz + dz, 4)
 
     for dx in far:
         for dz in far_z:
             if (dx, dz) != (0, 0):
                 greet(partner(dx, dz), mine)
     for dy in range(1, ny):
-        greet(me, (row_y + dy) % ny * 2 + core)
+        greet(me, lax.rem(row_y + dy, ny) * 2 + core)
     greet(me, row_y * 2 + 1 - core)
 
     def to_snd(refs, dest):
@@ -308,7 +308,7 @@
     def over_y(dy, slot):
         return pltpu.make_async_remote_copy(
             src_ref=send_y, dst_ref=recv_y.at[slot], send_sem=ss_y.at[dy], recv_sem=rs_y.at[slot],
-            device_id={"snd": me, "cell": (row_y + dy) % ny * 2 + core}, device_id_type=MESH,
+            device_id={"snd": me, "cell": lax.rem(row_y + dy, ny) * 2 + core}, device_id_type=MESH,
         )
 
     steps_y = {1: [], 2: [1], 4: [2, 1, 3]}[ny]
@@ -317,9 +317,9 @@
     sent(of_v)
     swap.wait_send()
     for dy in reversed(steps_y):
-        over_y(dy, (row_y + dy) % ny).wait_recv()
+        over_y(dy, lax.rem(row_y + dy, ny)).wait_recv()
     for dy in reversed(steps_y):
-        total = total + recv_y[(row_y + dy) % ny].astype(F32)
+        total = total + recv_y[lax.rem(row_y + dy, ny)].astype(F32)
     own = half // 128
     sigma = jnp.concatenate([sigma_ref[pl.ds(core * own + i, 1), :] for i in range(own)], axis=1)
     recv_w[core] = (total / (sigma * sigma)).astype(BF)
@@ -365,18 +365,22 @@
 
 
 def finish(carried_ref, spatial_ref, probes_ref, image_hbm, drop_hbm, image_ref, drop_ref, sems):
-    stores = [pltpu.make_async_copy(image_ref.at[t], image_hbm.at[t], sems.at[t]) for t in range(TT)]
+    stores = [
+        pltpu.make_async_copy(image_ref.at[pl.ds(t, 2)], image_hbm.at[pl.ds(t, 2)], sems.at[t]) for t in range(0, TT, 2)
+    ]
+    stores.append(pltpu.make_async_copy(drop_ref, drop_hbm, sems.at[TT]))
+    images = []
     for t in range(TT):
-        image = dot_nn(carried_ref[t], spatial_ref[t])
-        image_ref[t] = image
-        stores[t].start()
-        product = (probes_ref[t].astype(F32) * image).reshape(WEEKS, PROBES, CELLS)
+        images.append(dot_nn(carried_ref[t], spatial_ref[t]))
+        image_ref[t] = images[t]
+        if t % 2:
+            stores[t // 2].start()
+    for t in range(TT):
+        product = (probes_ref[t].astype(F32) * images[t]).reshape(WEEKS, PROBES, CELLS)
         drop_ref[t] = jnp.sum(product, axis=1) * (1.0 / PROBES)
-    last = pltpu.make_async_copy(drop_ref, drop_hbm, sems.at[TT])
-    last.start()
+    stores[-1].start()
     for store in stores:
         store.wait()
-    last.wait()
 
 
 def per_device(probes, spatial, rho, foot_tile, foot_week, footprint, sigma):

time: 33 us -> 33 us (level)
  no operation moved by 1% of the time
where the time goes in v7:
time: 33 us; the launch traced here: 32.9 us
  Pallas kernels  32.2 us (98%)
  between operations  0.67 us (2%)
    pallas_call x1, Pallas kernels, per_device(): pl.pallas_call(functools.partial(kernel, ns, nc, sound), out_shape=jax.Sh...  31.2 us
    pallas_call x1, Pallas kernels, per_device(): pl.pallas_call(finish, out_shape=(jax.ShapeDtypeStruct((TT, WEEKS * PROBE...  1.03 us

profile of v7, /device:TPU:1, one launch (start us, length us, event | category | flops | bytes accessed | tf_op | source)
XLA Modules:
  0.0 32.9 jit_solution(13908067572209182085)
XLA Ops:
  0.6 0.0 copy-start
  0.6 0.0 copy-start.1
  0.7 31.2 %shard_map.86.carried_ref = bf16[8,128,128]{2,1,0:T(8,128)(2,1)S(1)} custom-call(bf16[8,128,128]{2,1,0:T(8,128)(2,1)} %bitcast.6, bf16[8,128,128]{2,1,0:T(8,128)(2,1)} %spatial_ref.1, f32[8]{0:T(128)} %rho_hbm.1, s32[4,1024]{1,0:T(4,128)} %bitcast.9, s32[4,1024]{1,0:T(4,128)} %bitcast.10, bf16[4096,128]{1,0:T(8,128)(2,1)} %bitcast.8, f32[8,128]{1,0:T(8,128)} %bitcast.11), custom_call_target="tpu_custom_call" | custom-call | tf_op jit(solution)/shard_map/pallas_call | solution.py:403
  31.8 0.0 copy-done
  31.8 0.0 copy-done.1
  31.8 1.0 %shard_map.87 = (f32[8,128,128]{2,1,0:T(8,128)}, f32[8,4,128]{2,1,0:T(4,128)}) custom-call(bf16[8,128,128]{2,1,0:T(8,128)(2,1)S(1)} %shard_map.86.carried_ref, bf16[8,128,128]{2,1,0:T(8,128)(2,1)S(1)} %copy-done.1, bf16[8,128,128]{2,1,0:T(8,128)(2,1)S(1)} %bitcast.7), custom_call_target="tpu_custom_call" | custom-call | tf_op jit(solution)/shard_map/pallas_call | solution.py:443
Async XLA Ops:
  0.6 31.2 %copy-start = (bf16[8,4,32,128]{3,2,1,0:T(8,128)(2,1)S(1)}, bf16[8,4,32,128]{3,2,1,0:T(8,128)(2,1)}, u32[]{:S(2)}) copy-start(bf16[8,4,32,128]{3,2,1,0:T(8,128)(2,1)} %param.7) | copy-start | bytes 786436
  0.6 31.2 %copy-start.1 = (bf16[8,128,128]{2,1,0:T(8,128)(2,1)S(1)}, bf16[8,128,128]{2,1,0:T(8,128)(2,1)}, u32[]{:S(2)}) copy-start(bf16[8,128,128]{2,1,0:T(8,128)(2,1)} %spatial_ref.1) | copy-start | bytes 786436

commit v8 on v7

--- a/solution.py
+++ b/solution.py
@@ -79,7 +79,7 @@
     ns, nc, sound,
     probes_hbm, spatial_hbm, rho_hbm, tile_hbm, week_hbm, foot_hbm, sigma_hbm,
     carried_ref,
-    probes_ref, spatial_ref, rho_ref, tile_ref, week_ref, foot_ref, sigma_ref, order_ref, early_ref, ranks_ref, hot_ref, field_ref, wide_ref,
+    probes_ref, spatial_ref, rho_ref, tile_ref, week_ref, foot_ref, sigma_ref, order_ref, early_ref, ranks_ref, hot_ref, turned_ref, field_ref, wide_ref,
     send_f, recv_f, send_k, recv_k, send_v, recv_v, send_p, recv_p,
     send_c, recv_c, send_y, recv_y, recv_w,
     load_sem, ss_f, rs_f, ss_k, rs_k, ss_v, rs_v, ss_p, rs_p, ss_c, rs_c, ss_y, rs_y, ss_w, rs_w,
@@ -247,6 +247,7 @@
     for b in range(sound // 256):
         lanes = slice(256 * b, 256 * b + 256)
         hot_ref[:, lanes] = one_hot(doubled(order_ref[:, lanes]))
+        turned_ref[lanes, :] = hot_ref[:, lanes].T
 
     for load in loads[3:]:
         load.wait()
@@ -331,7 +332,7 @@
     share.wait_recv()
 
     weighted = jnp.concatenate([recv_w[0], recv_w[1]], axis=1)
-    backs = dot_nt(weighted, hot_ref[...])
+    backs = dot_nn(weighted, turned_ref[...])
     for x in range(groups):
         send_p[4 * x : 4 * x + 4] = packed(backs[:, 256 * x : 256 * x + 256])
     for dx in far:
@@ -417,6 +418,7 @@
             pltpu.VMEM((ns * TT, 128), F32),
             pltpu.VMEM((sound // 128, ns * 16, 512), BF),
             pltpu.VMEM((ns * SLOTS, sound), BF),
+            pltpu.VMEM((sound, ns * SLOTS), BF),
             pltpu.VMEM((TT // SIDE, WEEKS * PROBES, SIDE * CELLS), BF),
             pltpu.VMEM((ns * SLOTS, SIDE * CELLS), BF),
             pltpu.VMEM((ns, SLOTS, CELLS), BF),

time: 33 us -> 32.7 us (level)
  no operation moved by 1% of the time
where the time goes in v8:
time: 32.7 us; the launch traced here: 32.6 us
  Pallas kernels  31.9 us (98%)
  between operations  0.67 us (2%)
    pallas_call x1, Pallas kernels, per_device(): pl.pallas_call(functools.partial(kernel, ns, nc, sound), out_shape=jax.Sh...  30.9 us
    pallas_call x1, Pallas kernels, per_device(): pl.pallas_call(finish, out_shape=(jax.ShapeDtypeStruct((TT, WEEKS * PROBE...  1.02 us

profile of v8, /device:TPU:1, one launch (start us, length us, event | category | flops | bytes accessed | tf_op | source)
XLA Modules:
  0.0 32.6 jit_solution(2002468427575108372)
XLA Ops:
  0.6 0.0 copy-start
  0.6 0.0 copy-start.1
  0.7 30.9 %shard_map.86.carried_ref = bf16[8,128,128]{2,1,0:T(8,128)(2,1)S(1)} custom-call(bf16[8,128,128]{2,1,0:T(8,128)(2,1)} %bitcast.6, bf16[8,128,128]{2,1,0:T(8,128)(2,1)} %spatial_ref.1, f32[8]{0:T(128)} %rho_hbm.1, s32[4,1024]{1,0:T(4,128)} %bitcast.9, s32[4,1024]{1,0:T(4,128)} %bitcast.10, bf16[4096,128]{1,0:T(8,128)(2,1)} %bitcast.8, f32[8,128]{1,0:T(8,128)} %bitcast.11), custom_call_target="tpu_custom_call" | custom-call | tf_op jit(solution)/shard_map/pallas_call | solution.py:404
  31.6 0.0 copy-done
  31.6 0.0 copy-done.1
  31.6 1.0 %shard_map.87 = (f32[8,128,128]{2,1,0:T(8,128)}, f32[8,4,128]{2,1,0:T(4,128)}) custom-call(bf16[8,128,128]{2,1,0:T(8,128)(2,1)S(1)} %shard_map.86.carried_ref, bf16[8,128,128]{2,1,0:T(8,128)(2,1)S(1)} %copy-done.1, bf16[8,128,128]{2,1,0:T(8,128)(2,1)S(1)} %bitcast.7), custom_call_target="tpu_custom_call" | custom-call | tf_op jit(solution)/shard_map/pallas_call | solution.py:445
Async XLA Ops:
  0.6 30.9 %copy-start = (bf16[8,4,32,128]{3,2,1,0:T(8,128)(2,1)S(1)}, bf16[8,4,32,128]{3,2,1,0:T(8,128)(2,1)}, u32[]{:S(2)}) copy-start(bf16[8,4,32,128]{3,2,1,0:T(8,128)(2,1)} %param.7) | copy-start | bytes 786436
  0.6 30.9 %copy-start.1 = (bf16[8,128,128]{2,1,0:T(8,128)(2,1)S(1)}, bf16[8,128,128]{2,1,0:T(8,128)(2,1)}, u32[]{:S(2)}) copy-start(bf16[8,128,128]{2,1,0:T(8,128)(2,1)} %spatial_ref.1) | copy-start | bytes 786436

commit v9 on v8

--- a/solution.py
+++ b/solution.py
@@ -308,7 +308,7 @@
 
     def over_y(dy, slot):
         return pltpu.make_async_remote_copy(
-            src_ref=send_y, dst_ref=recv_y.at[slot], send_sem=ss_y.at[dy], recv_sem=rs_y.at[slot],
+            src_ref=send_y, dst_ref=recv_y.at[slot], send_sem=ss_y.at[dy], recv_sem=rs_y,
             device_id={"snd": me, "cell": lax.rem(row_y + dy, ny) * 2 + core}, device_id_type=MESH,
         )
 
@@ -317,8 +317,8 @@
         over_y(dy, row_y).start()
     sent(of_v)
     swap.wait_send()
-    for dy in reversed(steps_y):
-        over_y(dy, lax.rem(row_y + dy, ny)).wait_recv()
+    if ny > 1:
+        pltpu.make_async_copy(recv_y.at[pl.ds(0, ny - 1)], recv_y.at[pl.ds(0, ny - 1)], rs_y).wait()
     for dy in reversed(steps_y):
         total = total + recv_y[lax.rem(row_y + dy, ny)].astype(F32)
     own = half // 128
@@ -436,7 +436,7 @@
             pltpu.VMEM((2, PROBES, half), BF),
             dma(7),
             one, one, one, one, one, one, one, one,
-            one, one, dma(max(2, nc // 2)), dma(nc // 2), one, one,
+            one, one, dma(max(2, nc // 2)), one, one, one,
         ],
         compiler_params=pltpu.CompilerParams(
             collective_id=0, has_side_effects=True, vmem_limit_bytes=40 * 1024 * 1024

time: 32.7 us -> 32.7 us (level)
  no operation moved by 1% of the time
where the time goes in v9:
time: 32.7 us; the launch traced here: 32.6 us
  Pallas kernels  31.9 us (98%)
  between operations  0.67 us (2%)
    pallas_call x1, Pallas kernels, per_device(): pl.pallas_call(functools.partial(kernel, ns, nc, sound), out_shape=jax.Sh...  30.9 us
    pallas_call x1, Pallas kernels, per_device(): pl.pallas_call(finish, out_shape=(jax.ShapeDtypeStruct((TT, WEEKS * PROBE...  1.02 us

profile of v9, /device:TPU:1, one launch (start us, length us, event | category | flops | bytes accessed | tf_op | source)
XLA Modules:
  0.0 32.6 jit_solution(10838412338866785399)
XLA Ops:
  0.6 0.0 copy-start
  0.6 0.0 copy-start.1
  0.7 30.9 %shard_map.86.carried_ref = bf16[8,128,128]{2,1,0:T(8,128)(2,1)S(1)} custom-call(bf16[8,128,128]{2,1,0:T(8,128)(2,1)} %bitcast.6, bf16[8,128,128]{2,1,0:T(8,128)(2,1)} %spatial_ref.1, f32[8]{0:T(128)} %rho_hbm.1, s32[4,1024]{1,0:T(4,128)} %bitcast.9, s32[4,1024]{1,0:T(4,128)} %bitcast.10, bf16[4096,128]{1,0:T(8,128)(2,1)} %bitcast.8, f32[8,128]{1,0:T(8,128)} %bitcast.11), custom_call_target="tpu_custom_call" | custom-call | tf_op jit(solution)/shard_map/pallas_call | solution.py:404
  31.5 0.0 copy-done
  31.6 0.0 copy-done.1
  31.6 1.0 %shard_map.87 = (f32[8,128,128]{2,1,0:T(8,128)}, f32[8,4,128]{2,1,0:T(4,128)}) custom-call(bf16[8,128,128]{2,1,0:T(8,128)(2,1)S(1)} %shard_map.86.carried_ref, bf16[8,128,128]{2,1,0:T(8,128)(2,1)S(1)} %copy-done.1, bf16[8,128,128]{2,1,0:T(8,128)(2,1)S(1)} %bitcast.7), custom_call_target="tpu_custom_call" | custom-call | tf_op jit(solution)/shard_map/pallas_call | solution.py:445
Async XLA Ops:
  0.6 30.9 %copy-start = (bf16[8,4,32,128]{3,2,1,0:T(8,128)(2,1)S(1)}, bf16[8,4,32,128]{3,2,1,0:T(8,128)(2,1)}, u32[]{:S(2)}) copy-start(bf16[8,4,32,128]{3,2,1,0:T(8,128)(2,1)} %param.7) | copy-start | bytes 786436
  0.6 30.9 %copy-start.1 = (bf16[8,128,128]{2,1,0:T(8,128)(2,1)S(1)}, bf16[8,128,128]{2,1,0:T(8,128)(2,1)}, u32[]{:S(2)}) copy-start(bf16[8,128,128]{2,1,0:T(8,128)(2,1)} %spatial_ref.1) | copy-start | bytes 786436
